TPU v7x, 128 devices: a whole 4x4x4 slice. The times are simulated.
128 devices in a mesh: sub: 32 (over x, y, core), coarse: 4 (over z).
Axes of the slice: x: 4, y: 4, z: 4, core: 2. Of those that a mesh axis runs over, the one named last changes fastest.
Arguments:
- load: float32 [256, 6, 128, 256], P(('sub', 'coarse')), may hold values from -6 to 6
- schur: float32 [256, 768, 768], P(('sub', 'coarse')), as said below
- schur_inverse: float32 [256, 768, 768], P(('sub', 'coarse')), as said below
- basis: float32 [256, 768, 24], P(('sub', 'coarse')), may hold values from -1.25 to 1.25
- coarse_inverse: float32 [3584, 3584], P('coarse'), as said below
- partner_slot: int32 [256, 6], P(('sub', 'coarse')), may hold values from -1 to 1535, as said below
- edge_map: int32 [256, 6, 128], P(('sub', 'coarse')), may hold values from 0 to 127, as said below
- coarse_number: int32 [256, 6], P(('sub', 'coarse')), may hold values from 0 to 895, as said below
Outputs:
- solution: float32 [256, 6, 128, 256], P(('sub', 'coarse'))
- residual_next: float32 [256, 6, 128, 256], P(('sub', 'coarse'))
- direction_next: float32 [256, 6, 128, 256], P(('sub', 'coarse'))
Inputs may be any that keep to these rules, and one draw needn't show every extreme that they name: `partner_slot`: pairs are mutual: if face f of subdomain s names face g of subdomain t, then face g of t names face f of s. Each subdomain has exactly one face paired with a subdomain on the next device along sub+coarse and exactly one paired with a subdomain on the previous device, the first and last devices counting as adjacent; its other faces pair with subdomains on its own device or lie on the outer boundary. `edge_map`: on each paired face the two edge maps are permutations of 0 to 127 and inverse to each other. `coarse_number`: both sides of a paired face carry the same number; every number is used. `schur`: each matrix is symmetric positive definite. `schur_inverse`: each matrix is symmetric positive definite. `coarse_inverse`: symmetric positive definite.
All inputs are finite; a program needn't handle non-finite values.
Results may differ from a plain program's by a relative error of at most 0.00022.
Values sent between devices are 32-bit elements; how exact they have to be, the bound alone decides.
A program may use at most 128 MiB of HBM per device.

v0:
```python
import jax
import jax.numpy as jnp
from jax import lax
from jax.sharding import PartitionSpec as P


def extended(cells, sides, width):
    for axis, dim in sides:
        count = lax.axis_size(axis)
        head = lax.slice_in_dim(cells, 0, width, axis=dim)
        tail = lax.slice_in_dim(cells, cells.shape[dim] - width, cells.shape[dim], axis=dim)
        cells = jnp.concatenate(
            [
                lax.ppermute(tail, axis, [(i, (i + 1) % count) for i in range(count)]),
                cells,
                lax.ppermute(head, axis, [((i + 1) % count, i) for i in range(count)]),
            ],
            axis=dim,
        )
    return cells


def assemble(local_part, partner_slot, edge_map):
    blocks, face_count, edge_count, case_count = local_part.shape
    present = (partner_slot >= 0).astype(jnp.float32)[:, :, None, None]
    halo_pool = extended(local_part, ((("sub", "coarse"), 0),), blocks)
    all_slots = blocks * face_count * lax.axis_size(("sub", "coarse"))
    first_sub = (lax.axis_index(("sub", "coarse")) - 1) * blocks
    local_slots = jnp.clip(
        (partner_slot - first_sub * face_count) % all_slots, 0, 3 * blocks * face_count - 1
    )
    flat_index = (local_slots[:, :, None] * edge_count + edge_map).reshape(-1)
    flat_pool = halo_pool.reshape(3 * blocks * face_count * edge_count, case_count)
    partner_part = flat_pool[flat_index].reshape(local_part.shape)
    return local_part + present * partner_part


def local_inner(left, right, weight):
    return jnp.sum(weight[:, :, None, None] * left * right, axis=(0, 1, 2))


def global_inner(left, right, weight):
    return lax.psum(local_inner(left, right, weight), ("sub", "coarse"))


def coarse_solve(coarse_load, coarse_inverse):
    combined = lax.psum(coarse_load, ("sub", "coarse"))
    owned_rows = jnp.dot(coarse_inverse, combined, precision=lax.Precision.HIGHEST)
    return lax.all_gather(owned_rows, "coarse", axis=0, tiled=True)


def precondition(
    vector, weight, schur_inverse, basis, coarse_inverse, coarse_dofs, partner_slot, edge_map
):
    blocks, face_count, edge_count, case_count = vector.shape
    scaled = (weight[:, :, None, None] * vector).reshape(
        blocks, face_count * edge_count, case_count
    )
    local_part = jnp.einsum("snm,smr->snr", schur_inverse, scaled, precision=lax.Precision.HIGHEST)
    coarse_local = jnp.einsum("snc,snr->scr", basis, scaled, precision=lax.Precision.HIGHEST)
    coarse_load = (
        jnp.zeros((coarse_inverse.shape[1], case_count), jnp.float32)
        .at[coarse_dofs.reshape(-1)]
        .add(coarse_local.reshape(-1, case_count))
    )
    solved = coarse_solve(coarse_load, coarse_inverse)
    coarse_part = jnp.einsum(
        "snc,scr->snr", basis, solved[coarse_dofs], precision=lax.Precision.HIGHEST
    )
    combined = (local_part + coarse_part).reshape(vector.shape)
    return assemble(weight[:, :, None, None] * combined, partner_slot, edge_map)


def shards(
    load, schur, schur_inverse, basis, coarse_inverse, partner_slot, edge_map, coarse_number
):
    blocks, face_count, edge_count, case_count = load.shape
    per_face = basis.shape[2] // face_count
    weight = jnp.where(partner_slot >= 0, 0.5, 1.0).astype(jnp.float32)
    coarse_dofs = (
        coarse_number[:, :, None] * per_face + jnp.arange(per_face, dtype=jnp.int32)[None, None, :]
    ).reshape(blocks, face_count * per_face)
    residual = assemble(load, partner_slot, edge_map)
    direction = precondition(
        residual, weight, schur_inverse, basis, coarse_inverse, coarse_dofs, partner_slot, edge_map
    )
    product = jnp.einsum(
        "snm,smr->snr",
        schur,
        direction.reshape(blocks, face_count * edge_count, case_count),
        precision=lax.Precision.HIGHEST,
    )
    image = assemble(product.reshape(load.shape), partner_slot, edge_map)
    rz_first = global_inner(residual, direction, weight)
    alpha = rz_first / global_inner(direction, image, weight)
    solution = alpha * direction
    residual_next = residual - alpha * image
    preconditioned = precondition(
        residual_next,
        weight,
        schur_inverse,
        basis,
        coarse_inverse,
        coarse_dofs,
        partner_slot,
        edge_map,
    )
    beta = global_inner(residual_next, preconditioned, weight) / rz_first
    direction_next = preconditioned + beta * direction
    return (solution, residual_next, direction_next)


def solution(mesh):
    placed = (
        P(("sub", "coarse"), None, None, None),
        P(("sub", "coarse"), None, None),
        P(("sub", "coarse"), None, None),
        P(("sub", "coarse"), None, None),
        P("coarse", None),
        P(("sub", "coarse"), None),
        P(("sub", "coarse"), None, None),
        P(("sub", "coarse"), None),
    )
    return jax.shard_map(
        shards,
        mesh=mesh,
        in_specs=placed,
        out_specs=(
            P(("sub", "coarse"), None, None, None),
            P(("sub", "coarse"), None, None, None),
            P(("sub", "coarse"), None, None, None),
        ),
        check_vma=False,
    )
```

profile of v0, /device:TPU:1, one launch (start us, length us, event | category | flops | bytes accessed | tf_op | source)
XLA Modules:
  0.0 849.8 jit_solution(7533503122614806494)
XLA Ops:
  7.2 5.2 collective-permute-start.1
  16.3 30.7 %collective-permute-done.1 = f32[2,6,128,256]{3,2,1,0:T(8,128)S(1)} collective-permute-done((f32[2,6,128,256]{3,2,1,0:T(8,128)}, f32[2,6,128,256]{3,2,1,0:T(8,128)S(1)}, u32[]{:S(2)}, u32[]{:S(2)}) %collective-permute-start.1) | collective-permute-done | bytes 1572896 | tf_op jit(solution)/shard_map/ppermute | solution.py:16
  47.0 3.6 collective-permute-done
  50.6 3.9 pad_maximum_fusion
  54.5 7.1 gather_fusion
  61.6 1.7 broadcast_multiply_fusion.4
  64.3 2.9 scatter_custom_fusion
  67.4 151.4 %all-reduce.4.cloned.1.call-done = f32[3584,256]{1,0:T(8,128)} async-done(((f32[3584,256]{1,0:T(8,128)}), f32[3584,256]{1,0:T(8,128)}) %all-reduce.4.cloned.1.call-update) | async-done | bytes 3670032 | tf_op jit(solution)/shard_map/psum | solution.py:47
  218.8 27.6 %convolution_bitcast_fusion.2 = f32[896,256]{0,1:T(8,128)} fusion(f32[3584,256]{1,0:T(8,128)} %all-reduce.4.cloned.1.call-done, f32[896,3584]{1,0:T(8,128)} %param.12), kind=kOutput, calls=%fused_computation.29 | convolution fusion | flops 9865003008 | bytes 17432576 | tf_op jit(solution)/shard_map/dot_general | solution.py:48
  247.2 11.1 %fusion.9 = f32[2,256,768]{2,1,0:T(8,128)} fusion(f32[2,768,256]{2,1,0:T(8,128)S(1)} %bitcast.72, f32[2,768,768]{2,1,0:T(8,128)} %param.10), kind=kOutput, calls=%fused_computation.55 | convolution fusion | flops 3623878656 | bytes 7864320 | tf_op jit(solution)/shard_map/snm,smr->snr/dot_general | solution.py:59
  258.3 30.7 %all-gather.3.cloned.1.call-done = f32[3584,256]{0,1:T(8,128)} async-done(((f32[896,256]{0,1:T(8,128)}), f32[3584,256]{0,1:T(8,128)}) %all-gather.3.cloned.1.call-update) | async-done | bytes 3670032 | tf_op jit(solution)/shard_map/all_gather | solution.py:49
  289.0 5.1 copy.23
  294.2 2.7 gather_fusion.1
  296.8 2.8 add_bitcast_fusion.1
  299.7 1.6 copy.24
  301.3 1.6 broadcast_multiply_fusion.3
  304.8 33.5 %collective-permute-done.3 = f32[2,6,128,256]{3,2,1,0:T(8,128)S(1)} collective-permute-done((f32[2,6,128,256]{3,2,1,0:T(8,128)S(1)}, f32[2,6,128,256]{3,2,1,0:T(8,128)S(1)}, u32[]{:S(2)}, u32[]{:S(2)}) %collective-permute-start.3) | collective-permute-done | bytes 1572896 | tf_op jit(solution)/shard_map/ppermute | solution.py:16
  338.3 3.8 collective-permute-done.2
  342.1 2.4 pad_maximum_fusion.1
  344.6 7.0 gather_fusion.2
  351.5 3.0 copy.25
  354.6 8.3 convolution_bitcast_fusion
  362.8 3.1 copy.26
  367.4 3.6 multiply_reduce_fusion.2
  370.9 29.4 %collective-permute-done.5 = f32[2,6,128,256]{3,2,1,0:T(8,128)S(1)} collective-permute-done((f32[2,6,128,256]{3,2,1,0:T(8,128)}, f32[2,6,128,256]{3,2,1,0:T(8,128)S(1)}, u32[]{:S(2)}, u32[]{:S(2)}) %collective-permute-start.5) | collective-permute-done | bytes 1572896 | tf_op jit(solution)/shard_map/ppermute | solution.py:16
  400.3 3.7 collective-permute-done.4
  404.0 2.4 pad_maximum_fusion.2
  406.4 7.0 gather_fusion.3
  413.4 3.2 copy.27
  416.6 2.4 multiply_reduce_fusion.1
  419.0 64.0 %all-reduce = (f32[256]{0:T(256)S(1)}, f32[256]{0:T(256)S(1)}) all-reduce(f32[256]{0:T(256)S(1)} %get-tuple-element.7, f32[256]{0:T(256)S(1)} %multiply_reduce_fusion.1), channel_id=1, replica_groups=mesh['sub'=32,'coarse'=4] {'sub','coarse'}, use_global_device_ids=true, to_apply=%region_3.4 | all-reduce | flops 512 | bytes 4096 | tf_op jit(solution)/shard_map/psum | solution.py:43
  483.0 4.7 broadcast_multiply_fusion.2
  488.6 2.9 scatter_custom_fusion.1
  491.8 149.5 %all-reduce.6.cloned.1.call-done = f32[3584,256]{1,0:T(8,128)} async-done(((f32[3584,256]{1,0:T(8,128)}), f32[3584,256]{1,0:T(8,128)}) %all-reduce.6.cloned.1.call-update) | async-done | bytes 3670032 | tf_op jit(solution)/shard_map/psum | solution.py:47
  641.3 27.6 %convolution_bitcast_fusion.1 = f32[896,256]{0,1:T(8,128)} fusion(f32[3584,256]{1,0:T(8,128)} %all-reduce.6.cloned.1.call-done, f32[896,3584]{1,0:T(8,128)} %param.12), kind=kOutput, calls=%fused_computation.28 | convolution fusion | flops 9865003008 | bytes 17432576 | tf_op jit(solution)/shard_map/dot_general | solution.py:48
  668.9 9.7 %fusion.11 = f32[2,256,768]{2,1,0:T(8,128)S(1)} fusion(f32[2,768,256]{2,1,0:T(8,128)S(1)} %bitcast.74, f32[2,768,768]{2,1,0:T(8,128)} %param.10), kind=kOutput, calls=%fused_computation.57 | convolution fusion | flops 3623878656 | bytes 7864320 | tf_op jit(solution)/shard_map/snm,smr->snr/dot_general | solution.py:59
  678.6 32.9 %all-gather.5.cloned.1.call-done = f32[3584,256]{0,1:T(8,128)} async-done(((f32[896,256]{0,1:T(8,128)}), f32[3584,256]{0,1:T(8,128)}) %all-gather.5.cloned.1.call-update) | async-done | bytes 3670032 | tf_op jit(solution)/shard_map/all_gather | solution.py:49
  711.5 5.1 copy.29
  716.6 2.7 gather_fusion.4
  719.3 2.6 add_bitcast_fusion
  721.9 1.9 copy.30
  725.5 33.8 %collective-permute-done.7 = f32[2,6,128,256]{3,2,1,0:T(8,128)S(1)} collective-permute-done((f32[2,6,128,256]{3,2,1,0:T(8,128)S(1)}, f32[2,6,128,256]{3,2,1,0:T(8,128)S(1)}, u32[]{:S(2)}, u32[]{:S(2)}) %collective-permute-start.7) | collective-permute-done | bytes 1572896 | tf_op jit(solution)/shard_map/ppermute | solution.py:16
  759.3 3.7 collective-permute-done.6
  763.0 2.4 pad_maximum_fusion.3
  765.4 7.0 gather_fusion.5
  772.4 1.9 multiply_reduce_fusion
  774.3 64.5 %psum.39 = f32[256]{0:T(256)S(1)} all-reduce(f32[256]{0:T(256)S(1)} %multiply_reduce_fusion), channel_id=1, replica_groups=mesh['sub'=32,'coarse'=4] {'sub','coarse'}, use_global_device_ids=true, to_apply=%region_9.10 | all-reduce | flops 256 | bytes 2048 | tf_op jit(solution)/shard_map/psum | solution.py:43
  838.8 4.0 multiply_add_fusion
  (52 shorter events, 12.2 us)
Async XLA Ops:
  7.2 56.1 %copy-start = (f32[2,768,24]{1,2,0:T(8,128)S(1)}, f32[2,768,24]{1,2,0:T(8,128)}, u32[]{:S(2)}) copy-start(f32[2,768,24]{1,2,0:T(8,128)} %param.11) | copy-start | bytes 442372
  7.2 211.6 %all-reduce.4.cloned.1.call-start = ((), (), s32[]{:S(2)}) async-start(), calls=%async_computation | async-start | bytes 7340032 | tf_op jit(solution)/shard_map/psum | solution.py:47
  7.2 39.8 %collective-permute-start.1 = (f32[2,6,128,256]{3,2,1,0:T(8,128)}, f32[2,6,128,256]{3,2,1,0:T(8,128)S(1)}, u32[]{:S(2)}, u32[]{:S(2)}) collective-permute-start(f32[2,6,128,256]{3,2,1,0:T(8,128)} %param.8), channel_id=1, source_target_pairs={{1,0},{2,1},{3,2},{4,3},{5,4},{6,5},{7,6},{8,7},{9,8},{10,9},{11,1... | collective-permute-start | bytes 4718600 | tf_op jit(solution)/shard_map/ppermute | solution.py:16
  12.5 38.1 %collective-permute-start = (f32[2,6,128,256]{3,2,1,0:T(8,128)}, f32[2,6,128,256]{3,2,1,0:T(8,128)S(1)}, u32[]{:S(2)}, u32[]{:S(2)}) collective-permute-start(f32[2,6,128,256]{3,2,1,0:T(8,128)} %param.8), channel_id=1, source_target_pairs={{0,1},{1,2},{2,3},{3,4},{4,5},{5,6},{6,7},{7,8},{8,9},{9,10},{10,1... | collective-permute-start | bytes 4718600 | tf_op jit(solution)/shard_map/ppermute | solution.py:14
  54.5 7.1 copy-start.3
  67.1 221.9 %all-gather.3.cloned.1.call-start = ((), (), s32[]{:S(2)}) async-start(), calls=%async_computation.1 | async-start | bytes 4587520 | tf_op jit(solution)/shard_map/all_gather | solution.py:49
  246.4 394.9 %all-reduce.6.cloned.1.call-start = ((), (), s32[]{:S(2)}) async-start(), calls=%async_computation.2 | async-start | bytes 7340032 | tf_op jit(solution)/shard_map/psum | solution.py:47
  302.9 35.4 %collective-permute-start.3 = (f32[2,6,128,256]{3,2,1,0:T(8,128)S(1)}, f32[2,6,128,256]{3,2,1,0:T(8,128)S(1)}, u32[]{:S(2)}, u32[]{:S(2)}) collective-permute-start(f32[2,6,128,256]{3,2,1,0:T(8,128)S(1)} %broadcast_multiply_fusion.3), channel_id=1, source_target_pairs={{1,0},{2,1},{3,2},{4,3},{5,4},{6,5},{7,6},{8,7},{9,8},{10,9},{11,1... | collective-permute-start | bytes 4718600 | tf_op jit(solution)/shard_map/ppermute | solution.py:16
  304.1 38.1 %collective-permute-start.2 = (f32[2,6,128,256]{3,2,1,0:T(8,128)S(1)}, f32[2,6,128,256]{3,2,1,0:T(8,128)S(1)}, u32[]{:S(2)}, u32[]{:S(2)}) collective-permute-start(f32[2,6,128,256]{3,2,1,0:T(8,128)S(1)} %broadcast_multiply_fusion.3), channel_id=1, source_target_pairs={{0,1},{1,2},{2,3},{3,4},{4,5},{5,6},{6,7},{7,8},{8,9},{9,10},{10,1... | collective-permute-start | bytes 4718600 | tf_op jit(solution)/shard_map/ppermute | solution.py:14
  365.9 34.5 %collective-permute-start.5 = (f32[2,6,128,256]{3,2,1,0:T(8,128)}, f32[2,6,128,256]{3,2,1,0:T(8,128)S(1)}, u32[]{:S(2)}, u32[]{:S(2)}) collective-permute-start(f32[2,6,128,256]{3,2,1,0:T(8,128)} %bitcast.81), channel_id=1, source_target_pairs={{1,0},{2,1},{3,2},{4,3},{5,4},{6,5},{7,6},{8,7},{9,8},{10,9},{11,1... | collective-permute-start | bytes 4718600 | tf_op jit(solution)/shard_map/ppermute | solution.py:16
  365.9 38.1 %collective-permute-start.4 = (f32[2,6,128,256]{3,2,1,0:T(8,128)}, f32[2,6,128,256]{3,2,1,0:T(8,128)S(1)}, u32[]{:S(2)}, u32[]{:S(2)}) collective-permute-start(f32[2,6,128,256]{3,2,1,0:T(8,128)} %bitcast.82), channel_id=1, source_target_pairs={{0,1},{1,2},{2,3},{3,4},{4,5},{5,6},{6,7},{7,8},{8,9},{9,10},{10,1... | collective-permute-start | bytes 4718600 | tf_op jit(solution)/shard_map/ppermute | solution.py:14
  367.4 36.7 %copy-start.2 = (f32[2,768,256]{2,1,0:T(8,128)S(1)}, f32[2,768,256]{2,1,0:T(8,128)}, u32[]{:S(2)}) copy-start(f32[2,768,256]{2,1,0:T(8,128)} %copy.26) | copy-start | bytes 4718596
  413.4 3.2 copy-start.1
  491.5 220.0 %all-gather.5.cloned.1.call-start = ((), (), s32[]{:S(2)}) async-start(), calls=%async_computation.3 | async-start | bytes 4587520 | tf_op jit(solution)/shard_map/all_gather | solution.py:49
  723.9 35.4 %collective-permute-start.7 = (f32[2,6,128,256]{3,2,1,0:T(8,128)S(1)}, f32[2,6,128,256]{3,2,1,0:T(8,128)S(1)}, u32[]{:S(2)}, u32[]{:S(2)}) collective-permute-start(f32[2,6,128,256]{3,2,1,0:T(8,128)S(1)} %broadcast_multiply_fusion.1), channel_id=1, source_target_pairs={{1,0},{2,1},{3,2},{4,3},{5,4},{6,5},{7,6},{8,7},{9,8},{10,9},{11,1... | collective-permute-start | bytes 4718600 | tf_op jit(solution)/shard_map/ppermute | solution.py:16
  725.1 37.9 %collective-permute-start.6 = (f32[2,6,128,256]{3,2,1,0:T(8,128)S(1)}, f32[2,6,128,256]{3,2,1,0:T(8,128)S(1)}, u32[]{:S(2)}, u32[]{:S(2)}) collective-permute-start(f32[2,6,128,256]{3,2,1,0:T(8,128)S(1)} %broadcast_multiply_fusion.1), channel_id=1, source_target_pairs={{0,1},{1,2},{2,3},{3,4},{4,5},{5,6},{6,7},{7,8},{8,9},{9,10},{10,1... | collective-permute-start | bytes 4718600 | tf_op jit(solution)/shard_map/ppermute | solution.py:14
Sparse Core Ops, SparseCore 0:
  67.3 151.4 all-reduce.3
  246.5 42.4 all-gather.2
  491.6 149.5 all-reduce.5
  669.0 42.4 all-gather.4
where the time goes:
time: 854 us; the launch traced here: 850 us
  waiting for transfers between devices  507 us (59%)
  blocking collectives  129 us (15%)
  matrix products  91.6 us (11%)
  local copies, waits for them, and re-layouts  57 us (7%)
  other arithmetic  40.6 us (5%)
  between operations  14.3 us (2%)
  starting transfers between devices  10.9 us (1%)
    psum x2, waiting for transfers between devices, coarse_solve(): combined = lax.psum(coarse_load, ('sub', 'coarse'))  301 us
    psum x2, blocking collectives, global_inner(): return lax.psum(local_inner(left, right, weight), ('sub', 'coarse'))  129 us
    ppermute x4, waiting for transfers between devices, extended(): lax.ppermute(head, axis, [((i + 1) % count, i) for i in range(count)])  127 us
    all_gather x2, waiting for transfers between devices, coarse_solve(): return lax.all_gather(owned_rows, 'coarse', axis=0, tiled=True)  63.6 us
    dot_general x2, matrix products, coarse_solve(): jnp.dot(coarse_inverse, combined, precision=lax.Precision.HIGHEST)  55.2 us
    gather x4, local copies, waits for them, and re-layouts, assemble(): partner_part = flat_pool[flat_index].reshape(local_part.shape)  28 us
    dot_general x2, matrix products, precondition(): jnp.einsum('snm,smr->snr', schur_inverse, scaled, precision=lax.Precision...  20.8 us
  transfers between devices with their start and end apart: 12, of which 12 were waited for; matrix products, arithmetic and copies ran while one was open for 3% of the time, Pallas kernels for 0%

commit v1 on v0

v1 whole, which is shorter than its diff:
```python
import functools

import jax
import jax.numpy as jnp
from jax import lax
from jax.experimental import pallas as pl
from jax.experimental.pallas import tpu as pltpu
from jax.sharding import PartitionSpec as P

MESH = pl.DeviceIdType.MESH
F32 = jnp.float32
BF16 = jnp.bfloat16
FACES = 6
SUBS = 2
SLOTS = FACES * SUBS
NCF = 4
LANES = 128
CG = 8


def split(x):
    hi = x.astype(BF16)
    return hi, (x - hi.astype(F32)).astype(BF16)


def dot(a, b):
    return jnp.dot(a, b, preferred_element_type=F32)


def kernel(
    Q, Z, load, schur, sinv, basis_t, coarse, ps, em, cn,
    out_sol, out_r1, out_dn,
    vld, res, loc, dirn, prod, img, pre,
    hs0, hs1, hs2, hs3, hr0, hr1, hr2, hr3,
    sinv_hi, sinv_lo, schur_hi, schur_lo, c_hi, c_lo, s_stage, c_stage,
    hh, hl, perm, bt_hi, bt_lo, bcol, sp, spt,
    scat, gath, xbuf, xt, yt, xm, xb, y2,
    qb, qr, zb, zr, ob, zs0, zs1, arb, arr, arz0, arz1, cnz,
    in_sem, st_sem, ct_sem, out_sem, q_send, q_recv, h_send, h_recv,
):
    q = lax.axis_index("sub")
    z = lax.axis_index("coarse")
    E = vld.shape[1]
    NR = vld.shape[2]
    ZQ = Z * Q
    NCZ = c_hi.shape[0]
    NC0 = c_hi.shape[1]
    NF = NC0 // NCF
    NFZ = NF // Z
    RR = SLOTS * NCF * CG // LANES
    ndev = Q * Z
    me = q * Z + z
    nxt = lax.rem(me + 1, ndev)
    prv = lax.rem(me + ndev - 1, ndev)
    nxt_id = (nxt // Z, lax.rem(nxt, Z))
    prv_id = (prv // Z, lax.rem(prv, Z))

    def q_peer(k):
        return lax.rem(q + k, Q)

    def z_peer(k):
        return lax.rem(z + k, Z)

    load_copy = pltpu.make_async_copy(load, vld, in_sem)
    load_copy.start()

    def stager(src, rows, stage, sem):
        def copy(i, slot):
            return pltpu.make_async_copy(
                src.at[pl.ds(pl.multiple_of(i * rows, rows), rows), :], stage.at[slot], sem.at[slot]
            )
        return copy

    s_rows = s_stage.shape[1]
    c_rows = c_stage.shape[1]
    sinv_copy = stager(sinv, s_rows, s_stage, st_sem)
    schur_copy = stager(schur, s_rows, s_stage, st_sem)
    c_copy = stager(coarse, c_rows, c_stage, ct_sem)

    def first(copy):
        copy(0, 0).start()
        copy(1, 1).start()

    def convert(copy, stage, n, rows, hi_ref, lo_ref):
        def body(i, carry):
            slot = lax.rem(i, 2)
            copy(i, slot).wait()
            hi, lo = split(stage[slot])
            at = pl.ds(pl.multiple_of(i * rows, rows), rows)
            hi_ref[at, :] = hi
            lo_ref[at, :] = lo

            @pl.when(i + 2 < n)
            def _():
                copy(i + 2, slot).start()
            return carry
        lax.fori_loop(0, n, body, 0)

    first(sinv_copy)
    first(c_copy)

    barrier = pltpu.get_barrier_semaphore()

    def greet(device):
        pl.semaphore_signal(barrier, inc=1, device_id=device, device_id_type=MESH)

    lax.fori_loop(1, Q, lambda k, c: (greet((q_peer(k), z)), c)[1], 0)
    for k in range(1, Z):
        greet((q, z_peer(k)))
    greet(nxt_id)
    greet(prv_id)
    pl.semaphore_wait(barrier, Q + Z)

    lane8 = lax.broadcasted_iota(jnp.int32, (8, LANES), 1)

    def q_start(ph, src, dst, shared=False):
        def body(k, carry):
            p = q_peer(k)
            block = src if shared else src.at[pl.ds(pl.multiple_of(p * 8, 8), 8), :]
            pltpu.make_async_remote_copy(
                src_ref=block,
                dst_ref=dst.at[pl.ds(pl.multiple_of(q * 8, 8), 8), :],
                send_sem=q_send.at[ph], recv_sem=q_recv.at[ph],
                device_id=(p, z), device_id_type=MESH,
            ).start()
            return carry
        lax.fori_loop(1, Q, body, 0)
        mine = pl.ds(pl.multiple_of(q * 8, 8), 8)
        dst[mine, :] = src[...] if shared else src[mine, :]

    def q_wait(ph, dst, sems):
        every = dst.at[pl.ds(0, (Q - 1) * 8), :]
        pltpu.make_async_copy(every, every, sems.at[ph]).wait()

    def z_start(ph, src_of, dst):
        for k in range(1, Z):
            t = z_peer(k)
            pltpu.make_async_remote_copy(
                src_ref=src_of(t), dst_ref=dst,
                send_sem=q_send.at[ph], recv_sem=q_recv.at[ph],
                device_id=(q, t), device_id_type=MESH,
            ).start()

    def z_wait(ph, three, sems):
        pltpu.make_async_copy(three, three, sems.at[ph]).wait()

    row = jnp.zeros((8, LANES), F32)
    for k in range(SLOTS):
        row = jnp.where(lane8 == k, cn[k // FACES, k % FACES].astype(F32), row)
    arb[0] = row
    q_start(0, arb.at[0], arr.at[0], shared=True)

    def rel_of(k):
        p = ps[k // FACES, lax.rem(k, FACES)]
        rel = p - me * SLOTS
        rel = jnp.where(rel < -SLOTS, rel + ndev * SLOTS, rel)
        rel = jnp.where(rel >= 2 * SLOTS, rel - ndev * SLOTS, rel)
        return p, rel

    def weight_of(k):
        return jnp.where(ps[k // FACES, lax.rem(k, FACES)] >= 0, jnp.float32(0.5), jnp.float32(1.0))

    ups, downs = [], []
    for s in range(SUBS):
        up = jnp.int32(0)
        down = jnp.int32(0)
        for f in range(FACES):
            p, rel = rel_of(s * FACES + f)
            here = p >= 0
            up = jnp.where(here & (rel >= SLOTS), s * FACES + f, up)
            down = jnp.where(here & (rel < 0), s * FACES + f, down)
        ups.append(up)
        downs.append(down)

    def halo_start(h, v, send, recv):
        for s in range(SUBS):
            send[s] = v[ups[s]]
            send[SUBS + s] = v[downs[s]]
        for way, device in ((0, nxt_id), (1, prv_id)):
            part = pl.ds(way * SUBS, SUBS)
            pltpu.make_async_remote_copy(
                src_ref=send.at[part], dst_ref=recv.at[part],
                send_sem=h_send.at[h, way], recv_sem=h_recv.at[h, way],
                device_id=device, device_id_type=MESH,
            ).start()

    def halo_wait(h, recv, sems):
        for way in range(2):
            part = recv.at[pl.ds(way * SUBS, SUBS)]
            pltpu.make_async_copy(part, part, sems.at[h, way]).wait()

    def partner(k, v, recv):
        p, rel = rel_of(k)
        local = (rel >= 0) & (rel < SLOTS)
        inside = jnp.clip(rel, 0, SLOTS - 1)
        below = (rel + SLOTS >= FACES).astype(jnp.int32)
        above = SUBS + (rel - SLOTS >= FACES).astype(jnp.int32)
        outside = jnp.clip(jnp.where(rel < 0, below, above), 0, 2 * SUBS - 1)
        val = jnp.where(local, v[inside], recv[outside])
        hi, lo = split(val)
        return dot(perm[k], jnp.concatenate([hi, lo], axis=0))

    load_copy.wait()
    halo_start(0, vld, hs0, hr0)

    rows_e = lax.broadcasted_iota(jnp.int32, (E, E), 0)
    for k in range(SLOTS):
        line = em[k % FACES, pl.ds(k // FACES, 1), :]
        one = jnp.where(rows_e == line, jnp.float32(1.0), jnp.float32(0.0)).T
        one = jnp.where(ps[k // FACES, k % FACES] >= 0, one, jnp.zeros_like(one)).astype(BF16)
        perm[k] = jnp.concatenate([one, one], axis=1)

    NI = FACES * E
    NCL = FACES * NCF
    zrow = jnp.zeros((32 - NCL, NI), F32)
    for s in range(SUBS):
        b = basis_t[s]
        bh = b.astype(BF16).astype(F32)
        bl = b - bh
        bh = jnp.concatenate([bh, zrow], axis=0)
        bl = jnp.concatenate([bl, zrow], axis=0)
        bt_hi[s] = bh.astype(BF16)
        bt_lo[s] = bl.astype(BF16)
        bcol[s] = jnp.concatenate([bh, bh, bl, jnp.zeros_like(bl)], axis=0).T.astype(BF16)

    wide = RR * LANES
    i0 = lax.broadcasted_iota(jnp.int32, (wide, CG * LANES), 0)
    i1 = lax.broadcasted_iota(jnp.int32, (wide, CG * LANES), 1)
    target = (i0 & 7) * LANES + (i0 >> 7) * 16 + ((i0 & 127) >> 3)
    sp[...] = jnp.where(i1 == target, jnp.float32(1.0), jnp.float32(0.0)).astype(BF16)
    j0 = lax.broadcasted_iota(jnp.int32, (CG * LANES, wide), 0)
    j1 = lax.broadcasted_iota(jnp.int32, (CG * LANES, wide), 1)
    back = (j1 & 7) * LANES + (j1 >> 7) * 16 + ((j1 & 127) >> 3)
    spt[...] = jnp.where(j0 == back, jnp.float32(1.0), jnp.float32(0.0)).astype(BF16)

    q_wait(0, arr.at[0], q_recv)
    zmine = pl.ds(pl.multiple_of(z * Q, Q), Q)
    arz0[...] = arr[0, pl.ds(0, Q, stride=8), :]
    cnz[zmine, :] = arz0[...]
    z_start(1, lambda t: arz0, cnz.at[zmine, :])

    convert(sinv_copy, s_stage, SUBS * NI // s_rows, s_rows, sinv_hi, sinv_lo)
    first(schur_copy)

    z_wait(1, cnz.at[pl.ds(0, (Z - 1) * Q), :], q_recv)
    cns = cnz[...]
    cnt = cns.T if ZQ == LANES else jnp.concatenate([cns, jnp.zeros((LANES - ZQ, LANES), F32)], axis=0).T
    face0 = lax.broadcasted_iota(jnp.int32, (NF, ZQ), 0).astype(F32)
    face1 = lax.broadcasted_iota(jnp.int32, (ZQ, NFZ), 1).astype(F32) + (z * NFZ).astype(F32)
    for k in range(SLOTS):
        scat[:, k * ZQ:(k + 1) * ZQ] = jnp.where(
            face0 == cnt[k:k + 1, :ZQ], jnp.float32(1.0), jnp.float32(0.0)
        ).astype(BF16)
        gath[k] = jnp.where(
            cns[:, k:k + 1] == face1, jnp.float32(1.0), jnp.float32(0.0)
        ).astype(BF16)

    xbuf[...] = jnp.zeros_like(xbuf)

    def weigh(r_ref):
        def body(k, carry):
            hi, lo = split(weight_of(k) * r_ref[k])
            at = pl.ds(pl.multiple_of(k * E, E), E)
            hh[at, :] = hi
            hl[at, :] = lo
            return carry
        lax.fori_loop(0, SLOTS, body, 0)

    def local_mul(a_hi, a_lo, out):
        rows = 2 * E
        per = NI // rows

        def body(i, carry):
            at = pl.ds(pl.multiple_of(i * rows, rows), rows)
            sub = pl.ds(pl.multiple_of((i // per) * NI, NI), NI)
            hi = a_hi[at, :]
            top = hh[sub, :]
            acc = dot(hi, top) + dot(hi, hl[sub, :]) + dot(a_lo[at, :], top)
            out[2 * i] = acc[:E]
            out[2 * i + 1] = acc[E:]
            return carry
        lax.fori_loop(0, SUBS * per, body, 0)

    def forward_start(n):
        for s in range(SUBS):
            sub = pl.ds(s * NI, NI)
            top = hh[sub, :]
            x = dot(bt_hi[s], top) + dot(bt_hi[s], hl[sub, :]) + dot(bt_lo[s], top)
            xbuf[s * NCL:(s + 1) * NCL, :] = x[:NCL]
        xt[...] = xbuf[...].T
        acc = jnp.zeros((2 * Q, wide), F32)
        for c in range(CG):
            part = xt[pl.ds(c, Q, stride=CG), :]
            hi = part.astype(BF16).astype(F32)
            both = jnp.concatenate([hi, part - hi], axis=0).astype(BF16)
            acc += dot(both, spt[c * LANES:(c + 1) * LANES, :])
        acc = acc[:Q] + acc[Q:]
        b = qb.at[n]
        for r in range(RR):
            b[pl.ds(r, Q, stride=8), :] = acc[:, r * LANES:(r + 1) * LANES]
        for r in range(RR, 8):
            b[pl.ds(r, Q, stride=8), :] = jnp.zeros((Q, LANES), F32)
        q_start(2 + 4 * n, b, qr.at[n])

    def gather_start(n):
        q_wait(2 + 4 * n, qr.at[n], q_recv)
        for r in range(RR):
            part = qr[n, pl.ds(r, Q, stride=8), :]
            zb[n, r] = part
            zr[n, r, zmine, :] = part
        z_start(3 + 4 * n, lambda t: zb.at[n], zr.at[n, :, zmine, :])

    def coarse_product(n):
        z_wait(3 + 4 * n, zr.at[n, :, pl.ds(0, (Z - 1) * Q), :], q_recv)
        la = lax.broadcasted_iota(jnp.int32, (ZQ, LANES), 1) >> 5
        pieces = []
        for r in range(RR):
            part = zr[n, r]
            for a in range(NCF):
                hi, lo = split(jnp.where(la == a, part, jnp.float32(0.0)))
                pieces.append(jnp.concatenate([hi, lo], axis=1))
        slots = jnp.concatenate(pieces, axis=0)
        fb = NF // 7
        fa = lax.broadcasted_iota(jnp.int32, (fb, LANES), 1)

        def spread(i, carry):
            acc = dot(scat[pl.ds(pl.multiple_of(i * fb, fb), fb), :], slots)
            x = acc[:, :LANES] + acc[:, LANES:]
            x = x + pltpu.roll(x, 64, 1)
            x = x + pltpu.roll(x, 32, 1)
            hi = x.astype(BF16).astype(F32)
            v = jnp.where((fa >> 5) == 0, hi, jnp.where((fa >> 5) == 1, x - hi, jnp.float32(0.0)))
            for j in range(NCF):
                xm[pl.ds(j, fb, stride=NCF), :] = jnp.where(((fa >> 3) & 3) == j, v, jnp.float32(0.0))
            rows = pl.ds(pl.multiple_of(i * fb * NCF, fb * NCF), fb * NCF)
            xb[rows, :] = xm[...].astype(BF16)
            return carry
        lax.fori_loop(0, 7, spread, 0)
        yb = NCZ // 7

        def product(i, carry):
            rows = pl.ds(pl.multiple_of(i * yb, yb), yb)
            y = dot(c_hi[rows, :], xb[...]) + dot(c_lo[rows, :], xb[...])
            for shift in (64, 32, 16, 8):
                y = y + pltpu.roll(y, shift, 1)
            y2[rows, :] = y
            return carry
        lax.fori_loop(0, 7, product, 0)
        fj = (lax.broadcasted_iota(jnp.int32, (NFZ, LANES), 1) >> 3) & 3
        y = jnp.zeros((NFZ, LANES), F32)
        for j in range(NCF):
            y = jnp.where(fj == j, y2[pl.ds(j, NFZ, stride=NCF), :], y)
        hi, lo = split(y)
        both = jnp.concatenate([hi, lo], axis=1)
        for r in range(RR):
            o = jnp.zeros((ZQ, LANES), F32)
            for a in range(NCF):
                g = dot(gath[NCF * r + a], both)
                o = jnp.where(la == a, g[:, :LANES] + g[:, LANES:], o)
            ob[n, r] = o
        zs = (zs0, zs1)[n]
        zs[z] = ob[n, :, zmine, :]
        z_start(
            4 + 4 * n,
            lambda t: ob.at[n, :, pl.ds(pl.multiple_of(t * Q, Q), Q), :],
            zs.at[z],
        )

    def backward_start(n):
        zs = (zs0, zs1)[n]
        z_wait(4 + 4 * n, zs.at[pl.ds(0, Z - 1)], q_recv)
        b = qb.at[2 + n]
        for r in range(RR):
            tot = zs[0, r]
            for t in range(1, Z):
                tot = tot + zs[t, r]
            b[pl.ds(r, Q, stride=8), :] = tot
        for r in range(RR, 8):
            b[pl.ds(r, Q, stride=8), :] = jnp.zeros((Q, LANES), F32)
        q_start(5 + 4 * n, b, qr.at[2 + n])

    def backward_finish(n):
        q_wait(5 + 4 * n, qr.at[2 + n], q_recv)
        acc = jnp.zeros((2 * Q, CG * LANES), F32)
        for r in range(RR):
            part = qr[2 + n, pl.ds(r, Q, stride=8), :]
            hi = part.astype(BF16).astype(F32)
            both = jnp.concatenate([hi, part - hi], axis=0).astype(BF16)
            acc += dot(both, sp[r * LANES:(r + 1) * LANES, :])
        for c in range(CG):
            cols = slice(c * LANES, (c + 1) * LANES)
            yt[pl.ds(c, Q, stride=CG), :] = acc[:Q, cols] + acc[Q:, cols]
        return yt[...].T

    def add_coarse(y):
        pad = jnp.zeros((32 - NCL, NR), F32)
        for s in range(SUBS):
            ys = jnp.concatenate([y[s * NCL:(s + 1) * NCL], pad], axis=0)
            hi = ys.astype(BF16).astype(F32)
            lo = ys - hi
            cols = jnp.concatenate([hi, lo, hi, jnp.zeros_like(hi)], axis=0).astype(BF16)

            def body(f, carry):
                k = s * FACES + f
                at = pl.ds(pl.multiple_of(f * E, E), E)
                loc[k] = weight_of(k) * (loc[k] + dot(bcol[s, at, :], cols))
                return carry
            lax.fori_loop(0, FACES, body, 0)

    def fold(x):
        return x.reshape(E // 8, 8, NR).sum(axis=0)

    nh = max(1, NR // LANES)
    lw = min(NR, LANES)

    def sums_start(n, parts):
        b = arb.at[1 + n]
        b[...] = jnp.zeros((8, LANES), F32)
        for i, part in enumerate(parts):
            line = part.sum(axis=0, keepdims=True)
            for h in range(nh):
                b[pl.ds(i * nh + h, 1), 0:lw] = line[:, h * lw:(h + 1) * lw]
        q_start(10 + 2 * n, b, arr.at[1 + n], shared=True)

    def sums_finish(n, count):
        q_wait(10 + 2 * n, arr.at[1 + n], q_recv)
        tot = arr[1 + n].reshape(Q, 8, LANES).sum(axis=0)
        dst = (arz1.at[0], arz1.at[1])[n]
        arb[3 + n] = tot
        dst[z] = tot
        z_start(11 + 2 * n, lambda t: arb.at[3 + n], dst.at[z])
        z_wait(11 + 2 * n, dst.at[pl.ds(0, Z - 1)], q_recv)
        tot = dst[0]
        for t in range(1, Z):
            tot = tot + dst[t]
        return [
            jnp.concatenate([tot[i * nh + h:i * nh + h + 1, :lw] for h in range(nh)], axis=1)
            for i in range(count)
        ]

    zero8 = jnp.zeros((8, NR), F32)

    halo_wait(0, hr0, h_recv)

    def residual(k, carry):
        res[k] = vld[k] + partner(k, vld, hr0)
        return carry
    lax.fori_loop(0, SLOTS, residual, 0)

    weigh(res)
    forward_start(0)
    local_mul(sinv_hi, sinv_lo, loc)
    gather_start(0)
    convert(c_copy, c_stage, NCZ // c_rows, c_rows, c_hi, c_lo)
    coarse_product(0)
    convert(schur_copy, s_stage, SUBS * NI // s_rows, s_rows, schur_hi, schur_lo)
    backward_start(0)
    add_coarse(backward_finish(0))
    halo_start(1, loc, hs1, hr1)
    halo_wait(1, hr1, h_recv)

    def direction(k, acc):
        d = loc[k] + partner(k, loc, hr1)
        dirn[k] = d
        hi, lo = split(d)
        at = pl.ds(pl.multiple_of(k * E, E), E)
        hh[at, :] = hi
        hl[at, :] = lo
        return acc + fold(weight_of(k) * res[k] * d)
    rz_part = lax.fori_loop(0, SLOTS, direction, zero8)

    local_mul(schur_hi, schur_lo, prod)
    halo_start(2, prod, hs2, hr2)
    halo_wait(2, hr2, h_recv)

    def image(k, acc):
        m = prod[k] + partner(k, prod, hr2)
        img[k] = m
        return acc + fold(weight_of(k) * dirn[k] * m)
    da_part = lax.fori_loop(0, SLOTS, image, zero8)
    sums_start(0, [rz_part, da_part])
    rz, da = sums_finish(0, 2)
    alpha = rz / da

    def step(k, carry):
        vld[k] = alpha * dirn[k]
        res[k] = res[k] - alpha * img[k]
        return carry
    lax.fori_loop(0, SLOTS, step, 0)
    sol_copy = pltpu.make_async_copy(vld, out_sol, out_sem.at[0])
    sol_copy.start()
    r1_copy = pltpu.make_async_copy(res, out_r1, out_sem.at[1])
    r1_copy.start()

    weigh(res)
    forward_start(1)
    local_mul(sinv_hi, sinv_lo, loc)
    gather_start(1)
    coarse_product(1)
    backward_start(1)
    add_coarse(backward_finish(1))
    halo_start(3, loc, hs3, hr3)
    halo_wait(3, hr3, h_recv)

    def second(k, acc):
        d = loc[k] + partner(k, loc, hr3)
        pre[k] = d
        return acc + fold(weight_of(k) * res[k] * d)
    rz1_part = lax.fori_loop(0, SLOTS, second, zero8)
    sums_start(1, [rz1_part])
    (rz1,) = sums_finish(1, 1)
    beta = rz1 / rz

    def last(k, carry):
        pre[k] = pre[k] + beta * dirn[k]
        return carry
    lax.fori_loop(0, SLOTS, last, 0)
    dn_copy = pltpu.make_async_copy(pre, out_dn, out_sem.at[2])
    dn_copy.start()

    q_wait(0, arr.at[0], q_send)
    z_wait(1, cnz.at[pl.ds(0, (Z - 1) * Q), :], q_send)
    for n in range(2):
        q_wait(2 + 4 * n, qr.at[n], q_send)
        z_wait(3 + 4 * n, zr.at[n, :, pl.ds(0, (Z - 1) * Q), :], q_send)
        zs = (zs0, zs1)[n]
        z_wait(4 + 4 * n, zs.at[pl.ds(0, Z - 1)], q_send)
        q_wait(5 + 4 * n, qr.at[2 + n], q_send)
        q_wait(10 + 2 * n, arr.at[1 + n], q_send)
        z_wait(11 + 2 * n, arz1.at[n, pl.ds(0, Z - 1)], q_send)
    for h, recv in enumerate((hr0, hr1, hr2, hr3)):
        halo_wait(h, recv, h_send)
    sol_copy.wait()
    r1_copy.wait()
    dn_copy.wait()


def shards(Q, Z, load, schur, schur_inverse, basis, coarse_inverse, partner_slot, edge_map, coarse_number):
    E, NR = load.shape[2], load.shape[3]
    NI = FACES * E
    NCZ, NC0 = coarse_inverse.shape
    NF = NC0 // NCF
    ZQ = Z * Q
    RR = SLOTS * NCF * CG // LANES
    vec = pltpu.VMEM((SLOTS, E, NR), F32)
    halo = pltpu.VMEM((2 * SUBS, E, NR), F32)
    mat = pltpu.VMEM((SUBS * NI, NI), BF16)
    out = jax.ShapeDtypeStruct((SLOTS, E, NR), F32)
    anywhere = pl.BlockSpec(memory_space=pl.ANY)
    vmem = pl.BlockSpec(memory_space=pltpu.VMEM)
    smem = pl.BlockSpec(memory_space=pltpu.SMEM)
    outs = pl.pallas_call(
        functools.partial(kernel, Q, Z),
        out_shape=(out, out, out),
        in_specs=[anywhere, anywhere, anywhere, vmem, anywhere, smem, vmem, smem],
        out_specs=(anywhere, anywhere, anywhere),
        scratch_shapes=[vec] * 7 + [halo] * 8 + [mat] * 4 + [
            pltpu.VMEM((NCZ, NC0), BF16),
            pltpu.VMEM((NCZ, NC0), BF16),
            pltpu.VMEM((2, 2 * E, NI), F32),
            pltpu.VMEM((2, NCZ // 7, NC0), F32),
            pltpu.VMEM((SUBS * NI, NR), BF16),
            pltpu.VMEM((SUBS * NI, NR), BF16),
            pltpu.VMEM((SLOTS, E, 2 * E), BF16),
            pltpu.VMEM((SUBS, 32, NI), BF16),
            pltpu.VMEM((SUBS, 32, NI), BF16),
            pltpu.VMEM((SUBS, NI, LANES), BF16),
            pltpu.VMEM((RR * LANES, CG * LANES), BF16),
            pltpu.VMEM((CG * LANES, RR * LANES), BF16),
            pltpu.VMEM((NF, SLOTS * ZQ), BF16),
            pltpu.VMEM((SLOTS, ZQ, NF // Z), BF16),
            pltpu.VMEM((LANES, NR), F32),
            pltpu.VMEM((NR, LANES), F32),
            pltpu.VMEM((NR, LANES), F32),
            pltpu.VMEM((NC0 // 7, LANES), F32),
            pltpu.VMEM((NC0, LANES), BF16),
            pltpu.VMEM((NCZ, LANES), F32),
            pltpu.VMEM((4, Q * 8, LANES), F32),
            pltpu.VMEM((4, Q * 8, LANES), F32),
            pltpu.VMEM((2, RR, Q, LANES), F32),
            pltpu.VMEM((2, RR, ZQ, LANES), F32),
            pltpu.VMEM((2, RR, ZQ, LANES), F32),
            pltpu.VMEM((Z, RR, Q, LANES), F32),
            pltpu.VMEM((Z, RR, Q, LANES), F32),
            pltpu.VMEM((5, 8, LANES), F32),
            pltpu.VMEM((3, Q * 8, LANES), F32),
            pltpu.VMEM((Q, LANES), F32),
            pltpu.VMEM((2, Z, 8, LANES), F32),
            pltpu.VMEM((ZQ, LANES), F32),
            pltpu.SemaphoreType.DMA,
            pltpu.SemaphoreType.DMA((2,)),
            pltpu.SemaphoreType.DMA((2,)),
            pltpu.SemaphoreType.DMA((3,)),
            pltpu.SemaphoreType.DMA((14,)),
            pltpu.SemaphoreType.DMA((14,)),
            pltpu.SemaphoreType.DMA((4, 2)),
            pltpu.SemaphoreType.DMA((4, 2)),
        ],
        compiler_params=pltpu.CompilerParams(
            collective_id=0, has_side_effects=True, vmem_limit_bytes=60 * 1024 * 1024
        ),
    )(
        load.reshape(SLOTS, E, NR),
        schur.reshape(SUBS * NI, NI),
        schur_inverse.reshape(SUBS * NI, NI),
        jnp.swapaxes(basis, 1, 2),
        coarse_inverse,
        partner_slot,
        jnp.swapaxes(edge_map, 0, 1),
        coarse_number,
    )
    return tuple(o.reshape(load.shape) for o in outs)


def solution(mesh):
    both = ("sub", "coarse")
    placed = (
        P(both, None, None, None),
        P(both, None, None),
        P(both, None, None),
        P(both, None, None),
        P("coarse", None),
        P(both, None),
        P(both, None, None),
        P(both, None),
    )
    return jax.shard_map(
        functools.partial(shards, mesh.shape["sub"], mesh.shape["coarse"]),
        mesh=mesh,
        in_specs=placed,
        out_specs=(P(both, None, None, None),) * 3,
        check_vma=False,
    )
```

time: 854 us -> 149 us (0.17)
  waiting for transfers between devices: 507 us -> 0 us
  Pallas kernels: 0 us -> 142 us
  blocking collectives: 129 us -> 0 us
  matrix products: 91.6 us -> 0 us
  local copies, waits for them, and re-layouts: 57 us -> 5.89 us
  other arithmetic: 40.6 us -> 0 us
  between operations: 14.3 us -> 0.65 us
  starting transfers between devices: 10.9 us -> 0 us
    psum x2 -> x0, waiting for transfers between devices: 301 us -> none  [coarse_solve(): combined = lax.psum(coarse_load, ('sub', 'coarse'))]
    pallas_call x0 -> x1, Pallas kernels: none -> 142 us  [shards(): pl.pallas_call(functools.partial(kernel, Q, Z), out_shape=(out, out, out)...]
    ppermute x8 -> x0, waiting for transfers between devices: 142 us -> none  [the longest x4 127 us: extended(): lax.ppermute(head, axis, [((i + 1) % count, i) for i in range(count)])]
    psum x2 -> x0, blocking collectives: 129 us -> none  [global_inner(): return lax.psum(local_inner(left, right, weight), ('sub', 'coarse'))]
    dot_general x9 -> x0, matrix products: 91.6 us -> none  [the longest x2 55.2 us: coarse_solve(): jnp.dot(coarse_inverse, combined, precision=lax.Precision.HIGHEST)]
    all_gather x2 -> x0, waiting for transfers between devices: 63.6 us -> none  [coarse_solve(): return lax.all_gather(owned_rows, 'coarse', axis=0, tiled=True)]
    gather x6 -> x0, local copies, waits for them, and re-layouts: 33.3 us -> none  [the longest x4 28 us: assemble(): partner_part = flat_pool[flat_index].reshape(local_part.shape)]
    concatenate x4 -> x0, other arithmetic: 11.2 us -> none  [extended(): jnp.concatenate([lax.ppermute(tail, axis, [(i, (i + 1) % count) for i in...]
  transfers between devices with their start and end apart: 12 -> 0, of which waited for: 12 -> 0; matrix products, arithmetic and copies ran while one was open for 3% -> 0% of each run, Pallas kernels for 0% -> 0%
where the time goes in v1:
time: 149 us
  Pallas kernels  142 us (95%)
  local copies, waits for them, and re-layouts  5.89 us (4%)
    pallas_call x1, Pallas kernels, shards(): pl.pallas_call(functools.partial(kernel, Q, Z), out_shape=(out, out, out)...  142 us
    unnamed x7, local copies, waits for them, and re-layouts  5.89 us

profile of v1, /device:TPU:1, one launch (start us, length us, event | category | flops | bytes accessed | tf_op | source)
XLA Modules:
  0.0 148.9 jit_solution(9491147700960149100)
XLA Ops:
  0.6 142.4 %shard_map.103 = (f32[12,128,256]{2,1,0:T(8,128)}, f32[12,128,256]{2,1,0:T(8,128)}, f32[12,128,256]{2,1,0:T(8,128)}) custom-call(f32[12,128,256]{2,1,0:T(8,128)} %bitcast.10, f32[1536,768]{1,0:T(8,128)} %bitcast.8, f32[1536,768]{1,0:T(8,128)} %bitcast.9, f32[2,24,768]{2,1,0:T(8,128)} %bitcast.14, f32[896,3584]{1,0:T(8,128)} %coarse.1, s32[2,6]{1,0:T(2,128)} %ps.1, ...), custom_call_target="tpu_custom_call" | custom-call | tf_op jit(solution)/shard_map/pallas_call | solution.py:552
  143.0 0.0 copy-start.1
  143.0 2.8 %copy.14 = f32[2,6,128,256]{3,2,1,0:T(8,128)} copy(f32[2,6,128,256]{3,2,1,0:T(8,128)} %bitcast.13) | data formatting | bytes 3145728
  145.8 0.0 copy-done.1
  145.8 0.0 copy-start
  145.8 1.1 copy.15
  147.0 0.8 copy-done
  147.8 1.1 copy.16
Async XLA Ops:
  143.0 2.8 %copy-start.1 = (f32[12,128,256]{2,1,0:T(8,128)S(1)}, f32[12,128,256]{2,1,0:T(8,128)}, u32[]{:S(2)}) copy-start(f32[12,128,256]{2,1,0:T(8,128)} %get-tuple-element.7) | copy-start | bytes 4718596
  145.8 2.0 %copy-start = (f32[12,128,256]{2,1,0:T(8,128)S(1)}, f32[12,128,256]{2,1,0:T(8,128)}, u32[]{:S(2)}) copy-start(f32[12,128,256]{2,1,0:T(8,128)} %get-tuple-element.8) | copy-start | bytes 4718596

commit v2 on v1

--- a/solution.py
+++ b/solution.py
@@ -29,14 +29,14 @@
 
 def kernel(
     Q, Z, load, schur, sinv, basis_t, coarse, ps, em, cn,
-    out_sol, out_r1, out_dn,
-    vld, res, loc, dirn, prod, img, pre,
+    dirn, res, pre, out_ab,
+    vld, loc, prod, img,
     hs0, hs1, hs2, hs3, hr0, hr1, hr2, hr3,
     sinv_hi, sinv_lo, schur_hi, schur_lo, c_hi, c_lo, s_stage, c_stage,
     hh, hl, perm, bt_hi, bt_lo, bcol, sp, spt,
-    scat, gath, xbuf, xt, yt, xm, xb, y2,
+    fold4, scat, gath, xbuf, xt, yt, xm, xb, xf0, y2,
     qb, qr, zb, zr, ob, zs0, zs1, arb, arr, arz0, arz1, cnz,
-    in_sem, st_sem, ct_sem, out_sem, q_send, q_recv, h_send, h_recv,
+    in_sem, st_sem, ct_sem, q_send, q_recv, h_send, h_recv,
 ):
     q = lax.axis_index("sub")
     z = lax.axis_index("coarse")
@@ -61,6 +61,14 @@
     def z_peer(k):
         return lax.rem(z + k, Z)
 
+    owed = {}
+
+    def owe(key, ref, sem):
+        owed[key] = lambda: pltpu.make_async_copy(ref, ref, sem).wait()
+
+    def settle(*key):
+        owed.pop(key)()
+
     load_copy = pltpu.make_async_copy(load, vld, in_sem)
     load_copy.start()
 
@@ -80,6 +88,7 @@
     def first(copy):
         copy(0, 0).start()
         copy(1, 1).start()
+        owed[copy] = lambda: (copy(0, 0).wait(), copy(1, 1).wait())
 
     def convert(copy, stage, n, rows, hi_ref, lo_ref):
         def body(i, carry):
@@ -95,6 +104,7 @@
                 copy(i + 2, slot).start()
             return carry
         lax.fori_loop(0, n, body, 0)
+        owed.pop(copy)
 
     first(sinv_copy)
     first(c_copy)
@@ -109,13 +119,12 @@
         greet((q, z_peer(k)))
     greet(nxt_id)
     greet(prv_id)
-    pl.semaphore_wait(barrier, Q + Z)
 
     lane8 = lax.broadcasted_iota(jnp.int32, (8, LANES), 1)
 
     def q_start(ph, src, dst, shared=False):
-        def body(k, carry):
-            p = q_peer(k)
+        def body(i, carry):
+            p = q_peer(1 + lax.rem(i + Q // 2 - 1, Q - 1))
             block = src if shared else src.at[pl.ds(pl.multiple_of(p * 8, 8), 8), :]
             pltpu.make_async_remote_copy(
                 src_ref=block,
@@ -124,31 +133,23 @@
                 device_id=(p, z), device_id_type=MESH,
             ).start()
             return carry
-        lax.fori_loop(1, Q, body, 0)
+        lax.fori_loop(0, Q - 1, body, 0)
         mine = pl.ds(pl.multiple_of(q * 8, 8), 8)
         dst[mine, :] = src[...] if shared else src[mine, :]
-
-    def q_wait(ph, dst, sems):
         every = dst.at[pl.ds(0, (Q - 1) * 8), :]
-        pltpu.make_async_copy(every, every, sems.at[ph]).wait()
-
-    def z_start(ph, src_of, dst):
-        for k in range(1, Z):
+        owe((ph, "in"), every, q_recv.at[ph])
+        owe((ph, "out"), every, q_send.at[ph])
+
+    def z_start(ph, src_of, dst, three):
+        for k in sorted(range(1, Z), key=lambda k: -min(k, Z - k)):
             t = z_peer(k)
             pltpu.make_async_remote_copy(
                 src_ref=src_of(t), dst_ref=dst,
                 send_sem=q_send.at[ph], recv_sem=q_recv.at[ph],
                 device_id=(q, t), device_id_type=MESH,
             ).start()
-
-    def z_wait(ph, three, sems):
-        pltpu.make_async_copy(three, three, sems.at[ph]).wait()
-
-    row = jnp.zeros((8, LANES), F32)
-    for k in range(SLOTS):
-        row = jnp.where(lane8 == k, cn[k // FACES, k % FACES].astype(F32), row)
-    arb[0] = row
-    q_start(0, arb.at[0], arr.at[0], shared=True)
+        owe((ph, "in"), three, q_recv.at[ph])
+        owe((ph, "out"), three, q_send.at[ph])
 
     def rel_of(k):
         p = ps[k // FACES, lax.rem(k, FACES)]
@@ -183,11 +184,12 @@
                 send_sem=h_send.at[h, way], recv_sem=h_recv.at[h, way],
                 device_id=device, device_id_type=MESH,
             ).start()
-
-    def halo_wait(h, recv, sems):
-        for way in range(2):
-            part = recv.at[pl.ds(way * SUBS, SUBS)]
-            pltpu.make_async_copy(part, part, sems.at[h, way]).wait()
+            owe((h, way, "halo in"), recv.at[part], h_recv.at[h, way])
+            owe((h, way, "halo out"), recv.at[part], h_send.at[h, way])
+
+    def halo_wait(h):
+        settle(h, 0, "halo in")
+        settle(h, 1, "halo in")
 
     def partner(k, v, recv):
         p, rel = rel_of(k)
@@ -199,9 +201,6 @@
         val = jnp.where(local, v[inside], recv[outside])
         hi, lo = split(val)
         return dot(perm[k], jnp.concatenate([hi, lo], axis=0))
-
-    load_copy.wait()
-    halo_start(0, vld, hs0, hr0)
 
     rows_e = lax.broadcasted_iota(jnp.int32, (E, E), 0)
     for k in range(SLOTS):
@@ -223,26 +222,45 @@
         bt_lo[s] = bl.astype(BF16)
         bcol[s] = jnp.concatenate([bh, bh, bl, jnp.zeros_like(bl)], axis=0).T.astype(BF16)
 
-    wide = RR * LANES
-    i0 = lax.broadcasted_iota(jnp.int32, (wide, CG * LANES), 0)
-    i1 = lax.broadcasted_iota(jnp.int32, (wide, CG * LANES), 1)
+    i0 = lax.broadcasted_iota(jnp.int32, sp.shape, 0)
+    i1 = lax.broadcasted_iota(jnp.int32, sp.shape, 1)
     target = (i0 & 7) * LANES + (i0 >> 7) * 16 + ((i0 & 127) >> 3)
     sp[...] = jnp.where(i1 == target, jnp.float32(1.0), jnp.float32(0.0)).astype(BF16)
+    wide = RR * LANES
     j0 = lax.broadcasted_iota(jnp.int32, (CG * LANES, wide), 0)
     j1 = lax.broadcasted_iota(jnp.int32, (CG * LANES, wide), 1)
     back = (j1 & 7) * LANES + (j1 >> 7) * 16 + ((j1 & 127) >> 3)
     spt[...] = jnp.where(j0 == back, jnp.float32(1.0), jnp.float32(0.0)).astype(BF16)
 
-    q_wait(0, arr.at[0], q_recv)
+    m0 = lax.broadcasted_iota(jnp.int32, fold4.shape, 0)
+    m1 = lax.broadcasted_iota(jnp.int32, fold4.shape, 1)
+    fold4[...] = jnp.where(
+        ((m0 & 7) == (m1 & 7)) & ((m0 >> 8) == ((m1 >> 3) & 3)), jnp.float32(1.0), jnp.float32(0.0)
+    ).astype(BF16)
+    xbuf[...] = jnp.zeros_like(xbuf)
+
+    convert(sinv_copy, s_stage, SUBS * NI // s_rows, s_rows, sinv_hi, sinv_lo)
+    first(schur_copy)
+    load_copy.wait()
+    pl.semaphore_wait(barrier, Q + Z)
+    halo_start(0, vld, hs0, hr0)
+
+    row = jnp.zeros((8, LANES), F32)
+    for k in range(SLOTS):
+        row = jnp.where(lane8 == k, cn[k // FACES, k % FACES].astype(F32), row)
+    arb[0] = row
+    q_start(0, arb.at[0], arr.at[0], shared=True)
+
+    convert(c_copy, c_stage, NCZ // c_rows, c_rows, c_hi, c_lo)
+
+    settle(0, "in")
     zmine = pl.ds(pl.multiple_of(z * Q, Q), Q)
     arz0[...] = arr[0, pl.ds(0, Q, stride=8), :]
     cnz[zmine, :] = arz0[...]
-    z_start(1, lambda t: arz0, cnz.at[zmine, :])
-
-    convert(sinv_copy, s_stage, SUBS * NI // s_rows, s_rows, sinv_hi, sinv_lo)
-    first(schur_copy)
-
-    z_wait(1, cnz.at[pl.ds(0, (Z - 1) * Q), :], q_recv)
+    z_start(1, lambda t: arz0, cnz.at[zmine, :], cnz.at[pl.ds(0, (Z - 1) * Q), :])
+    convert(schur_copy, s_stage, SUBS * NI // s_rows, s_rows, schur_hi, schur_lo)
+
+    settle(1, "in")
     cns = cnz[...]
     cnt = cns.T if ZQ == LANES else jnp.concatenate([cns, jnp.zeros((LANES - ZQ, LANES), F32)], axis=0).T
     face0 = lax.broadcasted_iota(jnp.int32, (NF, ZQ), 0).astype(F32)
@@ -255,16 +273,12 @@
             cns[:, k:k + 1] == face1, jnp.float32(1.0), jnp.float32(0.0)
         ).astype(BF16)
 
-    xbuf[...] = jnp.zeros_like(xbuf)
-
-    def weigh(r_ref):
-        def body(k, carry):
-            hi, lo = split(weight_of(k) * r_ref[k])
-            at = pl.ds(pl.multiple_of(k * E, E), E)
-            hh[at, :] = hi
-            hl[at, :] = lo
-            return carry
-        lax.fori_loop(0, SLOTS, body, 0)
+
+    def put(k, x):
+        hi, lo = split(x)
+        at = pl.ds(pl.multiple_of(k * E, E), E)
+        hh[at, :] = hi
+        hl[at, :] = lo
 
     def local_mul(a_hi, a_lo, out):
         rows = 2 * E
@@ -303,15 +317,18 @@
         q_start(2 + 4 * n, b, qr.at[n])
 
     def gather_start(n):
-        q_wait(2 + 4 * n, qr.at[n], q_recv)
+        settle(2 + 4 * n, "in")
         for r in range(RR):
             part = qr[n, pl.ds(r, Q, stride=8), :]
             zb[n, r] = part
             zr[n, r, zmine, :] = part
-        z_start(3 + 4 * n, lambda t: zb.at[n], zr.at[n, :, zmine, :])
-
-    def coarse_product(n):
-        z_wait(3 + 4 * n, zr.at[n, :, pl.ds(0, (Z - 1) * Q), :], q_recv)
+        z_start(
+            3 + 4 * n, lambda t: zb.at[n], zr.at[n, :, zmine, :],
+            zr.at[n, :, pl.ds(0, (Z - 1) * Q), :],
+        )
+
+    def coarse_product(n, step=None):
+        settle(3 + 4 * n, "in")
         la = lax.broadcasted_iota(jnp.int32, (ZQ, LANES), 1) >> 5
         pieces = []
         for r in range(RR):
@@ -320,36 +337,29 @@
                 hi, lo = split(jnp.where(la == a, part, jnp.float32(0.0)))
                 pieces.append(jnp.concatenate([hi, lo], axis=1))
         slots = jnp.concatenate(pieces, axis=0)
-        fb = NF // 7
-        fa = lax.broadcasted_iota(jnp.int32, (fb, LANES), 1)
-
-        def spread(i, carry):
-            acc = dot(scat[pl.ds(pl.multiple_of(i * fb, fb), fb), :], slots)
-            x = acc[:, :LANES] + acc[:, LANES:]
-            x = x + pltpu.roll(x, 64, 1)
-            x = x + pltpu.roll(x, 32, 1)
-            hi = x.astype(BF16).astype(F32)
-            v = jnp.where((fa >> 5) == 0, hi, jnp.where((fa >> 5) == 1, x - hi, jnp.float32(0.0)))
-            for j in range(NCF):
-                xm[pl.ds(j, fb, stride=NCF), :] = jnp.where(((fa >> 3) & 3) == j, v, jnp.float32(0.0))
-            rows = pl.ds(pl.multiple_of(i * fb * NCF, fb * NCF), fb * NCF)
-            xb[rows, :] = xm[...].astype(BF16)
-            return carry
-        lax.fori_loop(0, 7, spread, 0)
-        yb = NCZ // 7
-
-        def product(i, carry):
-            rows = pl.ds(pl.multiple_of(i * yb, yb), yb)
-            y = dot(c_hi[rows, :], xb[...]) + dot(c_lo[rows, :], xb[...])
-            for shift in (64, 32, 16, 8):
-                y = y + pltpu.roll(y, shift, 1)
-            y2[rows, :] = y
-            return carry
-        lax.fori_loop(0, 7, product, 0)
-        fj = (lax.broadcasted_iota(jnp.int32, (NFZ, LANES), 1) >> 3) & 3
-        y = jnp.zeros((NFZ, LANES), F32)
+        fa = lax.broadcasted_iota(jnp.int32, (NF, LANES), 1)
+        acc = dot(scat[...], slots)
+        x = acc[:, :LANES] + acc[:, LANES:]
+        x = x + pltpu.roll(x, 64, 1)
+        x = x + pltpu.roll(x, 32, 1)
+        if step is not None:
+            x = xf0[...] - step() * x
+        xf0[...] = x
+        hi = x.astype(BF16).astype(F32)
+        v = jnp.where((fa >> 5) == 0, hi, jnp.where((fa >> 5) == 1, x - hi, jnp.float32(0.0)))
         for j in range(NCF):
-            y = jnp.where(fj == j, y2[pl.ds(j, NFZ, stride=NCF), :], y)
+            xm[pl.ds(j, NF, stride=NCF), :] = jnp.where(((fa >> 3) & 3) == j, v, jnp.float32(0.0))
+        xb[...] = xm[...].astype(BF16)
+        kc = NC0 // 7
+        acc = jnp.zeros((NCZ, LANES), F32)
+        for k in range(7):
+            cols = slice(k * kc, (k + 1) * kc)
+            acc += dot(c_hi[:, cols], xb[cols, :]) + dot(c_lo[:, cols], xb[cols, :])
+        y2[...] = acc
+        pieces = []
+        for j in range(NCF):
+            pieces.extend(split(y2[pl.ds(j, NFZ, stride=NCF), :]))
+        y = dot(jnp.concatenate(pieces, axis=1), fold4[...])
         hi, lo = split(y)
         both = jnp.concatenate([hi, lo], axis=1)
         for r in range(RR):
@@ -358,31 +368,35 @@
                 g = dot(gath[NCF * r + a], both)
                 o = jnp.where(la == a, g[:, :LANES] + g[:, LANES:], o)
             ob[n, r] = o
+        mine = xf0[pl.ds(pl.multiple_of(z * NFZ, 8) if NFZ % 8 == 0 else z * NFZ, NFZ), :]
+        energy = (mine * y).sum(axis=0, keepdims=True)
+        ob[n, RR] = jnp.where(la == 0, energy, jnp.float32(0.0))
         zs = (zs0, zs1)[n]
         zs[z] = ob[n, :, zmine, :]
         z_start(
             4 + 4 * n,
             lambda t: ob.at[n, :, pl.ds(pl.multiple_of(t * Q, Q), Q), :],
             zs.at[z],
+            zs.at[pl.ds(0, Z - 1)],
         )
 
     def backward_start(n):
         zs = (zs0, zs1)[n]
-        z_wait(4 + 4 * n, zs.at[pl.ds(0, Z - 1)], q_recv)
+        settle(4 + 4 * n, "in")
         b = qb.at[2 + n]
-        for r in range(RR):
+        for r in range(RR + 1):
             tot = zs[0, r]
             for t in range(1, Z):
                 tot = tot + zs[t, r]
             b[pl.ds(r, Q, stride=8), :] = tot
-        for r in range(RR, 8):
+        for r in range(RR + 1, 8):
             b[pl.ds(r, Q, stride=8), :] = jnp.zeros((Q, LANES), F32)
         q_start(5 + 4 * n, b, qr.at[2 + n])
 
     def backward_finish(n):
-        q_wait(5 + 4 * n, qr.at[2 + n], q_recv)
+        settle(5 + 4 * n, "in")
         acc = jnp.zeros((2 * Q, CG * LANES), F32)
-        for r in range(RR):
+        for r in range(RR + 1):
             part = qr[2 + n, pl.ds(r, Q, stride=8), :]
             hi = part.astype(BF16).astype(F32)
             both = jnp.concatenate([hi, part - hi], axis=0).astype(BF16)
@@ -422,117 +436,109 @@
                 b[pl.ds(i * nh + h, 1), 0:lw] = line[:, h * lw:(h + 1) * lw]
         q_start(10 + 2 * n, b, arr.at[1 + n], shared=True)
 
-    def sums_finish(n, count):
-        q_wait(10 + 2 * n, arr.at[1 + n], q_recv)
+    def sums_pass(n):
+        settle(10 + 2 * n, "in")
         tot = arr[1 + n].reshape(Q, 8, LANES).sum(axis=0)
-        dst = (arz1.at[0], arz1.at[1])[n]
         arb[3 + n] = tot
-        dst[z] = tot
-        z_start(11 + 2 * n, lambda t: arb.at[3 + n], dst.at[z])
-        z_wait(11 + 2 * n, dst.at[pl.ds(0, Z - 1)], q_recv)
-        tot = dst[0]
+        arz1[n, z] = tot
+        z_start(11 + 2 * n, lambda t: arb.at[3 + n], arz1.at[n, z], arz1.at[n, pl.ds(0, Z - 1)])
+
+    def sums_finish(n):
+        settle(11 + 2 * n, "in")
+        tot = arz1[n, 0]
         for t in range(1, Z):
-            tot = tot + dst[t]
-        return [
-            jnp.concatenate([tot[i * nh + h:i * nh + h + 1, :lw] for h in range(nh)], axis=1)
-            for i in range(count)
-        ]
+            tot = tot + arz1[n, t]
+        return tot
+
+    def cases(tile, i):
+        return jnp.concatenate([tile[i * nh + h:i * nh + h + 1, :lw] for h in range(nh)], axis=1)
+
+    def own_cases(tile):
+        row = jnp.where(q * CG >= LANES, tile[nh - 1:nh], tile[0:1])
+        row = jnp.broadcast_to(row, (8, LANES))
+        row = pltpu.roll(row, lax.rem(2 * LANES - q * CG + LANES, LANES), 1)
+        row = jnp.where(lane8 < CG, row, jnp.float32(0.0))
+        for shift in (8, 16, 32, 64):
+            row = row + pltpu.roll(row, shift, 1)
+        return row[0:1]
 
     zero8 = jnp.zeros((8, NR), F32)
 
-    halo_wait(0, hr0, h_recv)
+    halo_wait(0)
 
     def residual(k, carry):
-        res[k] = vld[k] + partner(k, vld, hr0)
+        r = vld[k] + partner(k, vld, hr0)
+        res[k] = r
+        put(k, weight_of(k) * r)
         return carry
     lax.fori_loop(0, SLOTS, residual, 0)
 
-    weigh(res)
     forward_start(0)
     local_mul(sinv_hi, sinv_lo, loc)
     gather_start(0)
-    convert(c_copy, c_stage, NCZ // c_rows, c_rows, c_hi, c_lo)
     coarse_product(0)
-    convert(schur_copy, s_stage, SUBS * NI // s_rows, s_rows, schur_hi, schur_lo)
     backward_start(0)
     add_coarse(backward_finish(0))
     halo_start(1, loc, hs1, hr1)
-    halo_wait(1, hr1, h_recv)
+    halo_wait(1)
 
     def direction(k, acc):
         d = loc[k] + partner(k, loc, hr1)
         dirn[k] = d
-        hi, lo = split(d)
-        at = pl.ds(pl.multiple_of(k * E, E), E)
-        hh[at, :] = hi
-        hl[at, :] = lo
+        put(k, d)
         return acc + fold(weight_of(k) * res[k] * d)
     rz_part = lax.fori_loop(0, SLOTS, direction, zero8)
 
     local_mul(schur_hi, schur_lo, prod)
     halo_start(2, prod, hs2, hr2)
-    halo_wait(2, hr2, h_recv)
+    halo_wait(2)
 
     def image(k, acc):
         m = prod[k] + partner(k, prod, hr2)
         img[k] = m
-        return acc + fold(weight_of(k) * dirn[k] * m)
+        wm = weight_of(k) * m
+        put(k, wm)
+        return acc + fold(dirn[k] * wm)
     da_part = lax.fori_loop(0, SLOTS, image, zero8)
+
+    forward_start(1)
     sums_start(0, [rz_part, da_part])
-    rz, da = sums_finish(0, 2)
-    alpha = rz / da
-
-    def step(k, carry):
-        vld[k] = alpha * dirn[k]
-        res[k] = res[k] - alpha * img[k]
+    gather_start(1)
+    sums_pass(0)
+    tot = sums_finish(0)
+    rz = cases(tot, 0)
+    alpha = rz / cases(tot, 1)
+    coarse_product(1, lambda: own_cases(tot[:nh] / tot[nh:2 * nh]))
+
+    def advance(k, carry):
+        r = res[k] - alpha * img[k]
+        res[k] = r
+        put(k, weight_of(k) * r)
         return carry
-    lax.fori_loop(0, SLOTS, step, 0)
-    sol_copy = pltpu.make_async_copy(vld, out_sol, out_sem.at[0])
-    sol_copy.start()
-    r1_copy = pltpu.make_async_copy(res, out_r1, out_sem.at[1])
-    r1_copy.start()
-
-    weigh(res)
-    forward_start(1)
+    lax.fori_loop(0, SLOTS, advance, 0)
+
     local_mul(sinv_hi, sinv_lo, loc)
-    gather_start(1)
-    coarse_product(1)
     backward_start(1)
-    add_coarse(backward_finish(1))
+
+    def energies(k, acc):
+        return acc + fold(weight_of(k) * res[k] * loc[k])
+    sums_start(1, [lax.fori_loop(0, SLOTS, energies, zero8)])
+    y = backward_finish(1)
+    coarse_energy = y[SUBS * NCL:SUBS * NCL + NCF].sum(axis=0, keepdims=True)
+    add_coarse(y)
     halo_start(3, loc, hs3, hr3)
-    halo_wait(3, hr3, h_recv)
-
-    def second(k, acc):
-        d = loc[k] + partner(k, loc, hr3)
-        pre[k] = d
-        return acc + fold(weight_of(k) * res[k] * d)
-    rz1_part = lax.fori_loop(0, SLOTS, second, zero8)
-    sums_start(1, [rz1_part])
-    (rz1,) = sums_finish(1, 1)
-    beta = rz1 / rz
-
-    def last(k, carry):
-        pre[k] = pre[k] + beta * dirn[k]
+    sums_pass(1)
+    beta = (cases(sums_finish(1), 0) + coarse_energy) / rz
+    halo_wait(3)
+
+    def second(k, carry):
+        pre[k] = loc[k] + partner(k, loc, hr3)
         return carry
-    lax.fori_loop(0, SLOTS, last, 0)
-    dn_copy = pltpu.make_async_copy(pre, out_dn, out_sem.at[2])
-    dn_copy.start()
-
-    q_wait(0, arr.at[0], q_send)
-    z_wait(1, cnz.at[pl.ds(0, (Z - 1) * Q), :], q_send)
-    for n in range(2):
-        q_wait(2 + 4 * n, qr.at[n], q_send)
-        z_wait(3 + 4 * n, zr.at[n, :, pl.ds(0, (Z - 1) * Q), :], q_send)
-        zs = (zs0, zs1)[n]
-        z_wait(4 + 4 * n, zs.at[pl.ds(0, Z - 1)], q_send)
-        q_wait(5 + 4 * n, qr.at[2 + n], q_send)
-        q_wait(10 + 2 * n, arr.at[1 + n], q_send)
-        z_wait(11 + 2 * n, arz1.at[n, pl.ds(0, Z - 1)], q_send)
-    for h, recv in enumerate((hr0, hr1, hr2, hr3)):
-        halo_wait(h, recv, h_send)
-    sol_copy.wait()
-    r1_copy.wait()
-    dn_copy.wait()
+    lax.fori_loop(0, SLOTS, second, 0)
+    out_ab[...] = jnp.concatenate([alpha, beta, jnp.zeros((6, NR), F32)], axis=0)
+
+    for wait in list(owed.values()):
+        wait()
 
 
 def shards(Q, Z, load, schur, schur_inverse, basis, coarse_inverse, partner_slot, edge_map, coarse_number):
@@ -545,16 +551,16 @@
     vec = pltpu.VMEM((SLOTS, E, NR), F32)
     halo = pltpu.VMEM((2 * SUBS, E, NR), F32)
     mat = pltpu.VMEM((SUBS * NI, NI), BF16)
-    out = jax.ShapeDtypeStruct((SLOTS, E, NR), F32)
+    out = pltpu.VMEM((SLOTS, E, NR), F32)
     anywhere = pl.BlockSpec(memory_space=pl.ANY)
     vmem = pl.BlockSpec(memory_space=pltpu.VMEM)
     smem = pl.BlockSpec(memory_space=pltpu.SMEM)
-    outs = pl.pallas_call(
+    direction, residual, preconditioned, ratios = pl.pallas_call(
         functools.partial(kernel, Q, Z),
-        out_shape=(out, out, out),
+        out_shape=(out, out, out, jax.ShapeDtypeStruct((8, NR), F32)),
         in_specs=[anywhere, anywhere, anywhere, vmem, anywhere, smem, vmem, smem],
-        out_specs=(anywhere, anywhere, anywhere),
-        scratch_shapes=[vec] * 7 + [halo] * 8 + [mat] * 4 + [
+        out_specs=(vmem, vmem, vmem, vmem),
+        scratch_shapes=[vec] * 4 + [halo] * 8 + [mat] * 4 + [
             pltpu.VMEM((NCZ, NC0), BF16),
             pltpu.VMEM((NCZ, NC0), BF16),
             pltpu.VMEM((2, 2 * E, NI), F32),
@@ -565,23 +571,25 @@
             pltpu.VMEM((SUBS, 32, NI), BF16),
             pltpu.VMEM((SUBS, 32, NI), BF16),
             pltpu.VMEM((SUBS, NI, LANES), BF16),
-            pltpu.VMEM((RR * LANES, CG * LANES), BF16),
+            pltpu.VMEM(((RR + 1) * LANES, CG * LANES), BF16),
             pltpu.VMEM((CG * LANES, RR * LANES), BF16),
+            pltpu.VMEM((2 * NCF * LANES, LANES), BF16),
             pltpu.VMEM((NF, SLOTS * ZQ), BF16),
             pltpu.VMEM((SLOTS, ZQ, NF // Z), BF16),
             pltpu.VMEM((LANES, NR), F32),
             pltpu.VMEM((NR, LANES), F32),
             pltpu.VMEM((NR, LANES), F32),
-            pltpu.VMEM((NC0 // 7, LANES), F32),
+            pltpu.VMEM((NC0, LANES), F32),
             pltpu.VMEM((NC0, LANES), BF16),
+            pltpu.VMEM((NF, LANES), F32),
             pltpu.VMEM((NCZ, LANES), F32),
             pltpu.VMEM((4, Q * 8, LANES), F32),
             pltpu.VMEM((4, Q * 8, LANES), F32),
             pltpu.VMEM((2, RR, Q, LANES), F32),
             pltpu.VMEM((2, RR, ZQ, LANES), F32),
-            pltpu.VMEM((2, RR, ZQ, LANES), F32),
-            pltpu.VMEM((Z, RR, Q, LANES), F32),
-            pltpu.VMEM((Z, RR, Q, LANES), F32),
+            pltpu.VMEM((2, RR + 1, ZQ, LANES), F32),
+            pltpu.VMEM((Z, RR + 1, Q, LANES), F32),
+            pltpu.VMEM((Z, RR + 1, Q, LANES), F32),
             pltpu.VMEM((5, 8, LANES), F32),
             pltpu.VMEM((3, Q * 8, LANES), F32),
             pltpu.VMEM((Q, LANES), F32),
@@ -590,14 +598,13 @@
             pltpu.SemaphoreType.DMA,
             pltpu.SemaphoreType.DMA((2,)),
             pltpu.SemaphoreType.DMA((2,)),
-            pltpu.SemaphoreType.DMA((3,)),
             pltpu.SemaphoreType.DMA((14,)),
             pltpu.SemaphoreType.DMA((14,)),
             pltpu.SemaphoreType.DMA((4, 2)),
             pltpu.SemaphoreType.DMA((4, 2)),
         ],
         compiler_params=pltpu.CompilerParams(
-            collective_id=0, has_side_effects=True, vmem_limit_bytes=60 * 1024 * 1024
+            collective_id=0, has_side_effects=True, vmem_limit_bytes=56 * 1024 * 1024
         ),
     )(
         load.reshape(SLOTS, E, NR),
@@ -609,7 +616,11 @@
         jnp.swapaxes(edge_map, 0, 1),
         coarse_number,
     )
-    return tuple(o.reshape(load.shape) for o in outs)
+    alpha, beta = ratios[0], ratios[1]
+    return tuple(
+        o.reshape(load.shape)
+        for o in (alpha * direction, residual, preconditioned + beta * direction)
+    )
 
 
 def solution(mesh):

time: 149 us -> 128 us (0.86)
  Pallas kernels: 142 us -> 123 us
  local copies, waits for them, and re-layouts: 5.89 us -> 1.92 us
  other arithmetic: 0 us -> 2.02 us
    pallas_call x1, Pallas kernels: 142 us -> 123 us  [shards(): pl.pallas_call(functools.partial(kernel, Q, Z), out_shape=(out, out, out,...]
    unnamed x7 -> x1, local copies, waits for them, and re-layouts: 5.89 us -> 1.14 us
    add x0 -> x1, other arithmetic: none -> 2.02 us  [shards(): preconditioned + beta * direction]
where the time goes in v2:
time: 128 us; the launch traced here: 127 us
  Pallas kernels  123 us (96%)
  other arithmetic  2.02 us (2%)
  local copies, waits for them, and re-layouts  1.92 us (2%)
    pallas_call x1, Pallas kernels, shards(): pl.pallas_call(functools.partial(kernel, Q, Z), out_shape=(out, out, out,...  123 us

profile of v2, /device:TPU:1, one launch (start us, length us, event | category | flops | bytes accessed | tf_op | source)
XLA Modules:
  0.0 127.3 jit_solution(2853858459868332733)
XLA Ops:
  0.6 122.7 %shard_map.103 = (f32[12,128,256]{2,1,0:T(8,128)S(1)}, f32[12,128,256]{2,1,0:T(8,128)S(1)}, f32[12,128,256]{2,1,0:T(8,128)S(1)}, f32[8,256]{1,0:T(8,128)}) custom-call(f32[12,128,256]{2,1,0:T(8,128)} %bitcast.13, f32[1536,768]{1,0:T(8,128)} %bitcast.11, f32[1536,768]{1,0:T(8,128)} %bitcast.12, f32[2,24,768]{2,1,0:T(8,128)} %bitcast.16, f32[896,3584]{1,0:T(8,128)} %coarse.1, ...), custom_call_target="tpu_custom_call" | custom-call | tf_op jit(solution)/shard_map/pallas_call | solution.py:558
  123.4 0.8 fusion
  124.1 2.0 %multiply_add_fusion = (f32[12,128,256]{2,1,0:T(8,128)}, f32[12,128,256]{2,1,0:T(8,128)}) fusion(f32[12,128,256]{2,1,0:T(8,128)S(1)} %get-tuple-element.10, f32[12,128,256]{2,1,0:T(8,128)S(1)} %get-tuple-element.8, f32[256]{0:T(256)S(1)} %bitcast.18, f32[256]{0:T(256)S(1)} %bitcast.19), kind=kLoop, calls=%fused_computation | loop fusion | flops 1179648 | bytes 6293504 | tf_op jit(solution)/shard_map/add | solution.py:622
  126.2 1.1 copy.12

commit v3 on v2

--- a/solution.py
+++ b/solution.py
@@ -29,11 +29,11 @@
 
 def kernel(
     Q, Z, load, schur, sinv, basis_t, coarse, ps, em, cn,
-    dirn, res, pre, out_ab,
-    vld, loc, prod, img,
+    dirn, res, img, pre, out_alpha, out_beta,
+    vld, loc, prod,
     hs0, hs1, hs2, hs3, hr0, hr1, hr2, hr3,
     sinv_hi, sinv_lo, schur_hi, schur_lo, c_hi, c_lo, s_stage, c_stage,
-    hh, hl, perm, bt_hi, bt_lo, bcol, sp, spt,
+    hh, hl, perm, bt_hi, bt_lo, bcol, bface, bpart, bs, br, gs, gr, ys, yr, sp, spt,
     fold4, scat, gath, xbuf, xt, yt, xm, xb, xf0, y2,
     qb, qr, zb, zr, ob, zs0, zs1, arb, arr, arz0, arz1, cnz,
     in_sem, st_sem, ct_sem, q_send, q_recv, h_send, h_recv,
@@ -173,12 +173,9 @@
         ups.append(up)
         downs.append(down)
 
-    def halo_start(h, v, send, recv):
-        for s in range(SUBS):
-            send[s] = v[ups[s]]
-            send[SUBS + s] = v[downs[s]]
+    def pair_start(h, send, recv, count):
         for way, device in ((0, nxt_id), (1, prv_id)):
-            part = pl.ds(way * SUBS, SUBS)
+            part = pl.ds(way * count, count)
             pltpu.make_async_remote_copy(
                 src_ref=send.at[part], dst_ref=recv.at[part],
                 send_sem=h_send.at[h, way], recv_sem=h_recv.at[h, way],
@@ -187,20 +184,35 @@
             owe((h, way, "halo in"), recv.at[part], h_recv.at[h, way])
             owe((h, way, "halo out"), recv.at[part], h_send.at[h, way])
 
+    def halo_start(h, v, send, recv):
+        for s in range(SUBS):
+            send[s] = v[ups[s]]
+            send[SUBS + s] = v[downs[s]]
+        pair_start(h, send, recv, SUBS)
+
     def halo_wait(h):
         settle(h, 0, "halo in")
         settle(h, 1, "halo in")
 
-    def partner(k, v, recv):
+    def place_of(k):
         p, rel = rel_of(k)
         local = (rel >= 0) & (rel < SLOTS)
         inside = jnp.clip(rel, 0, SLOTS - 1)
         below = (rel + SLOTS >= FACES).astype(jnp.int32)
         above = SUBS + (rel - SLOTS >= FACES).astype(jnp.int32)
-        outside = jnp.clip(jnp.where(rel < 0, below, above), 0, 2 * SUBS - 1)
-        val = jnp.where(local, v[inside], recv[outside])
+        return local, inside, jnp.clip(jnp.where(rel < 0, below, above), 0, 2 * SUBS - 1)
+
+    def permute(k, val):
         hi, lo = split(val)
         return dot(perm[k], jnp.concatenate([hi, lo], axis=0))
+
+    def partner(k, v, recv):
+        local, inside, outside = place_of(k)
+        return permute(k, jnp.where(local, v[inside], recv[outside]))
+
+    def partner_here(k, v):
+        local, inside, outside = place_of(k)
+        return permute(k, jnp.where(local, v[inside], jnp.float32(0.0)))
 
     rows_e = lax.broadcasted_iota(jnp.int32, (E, E), 0)
     for k in range(SLOTS):
@@ -211,6 +223,27 @@
 
     NI = FACES * E
     NCL = FACES * NCF
+    convert(sinv_copy, s_stage, SUBS * NI // s_rows, s_rows, sinv_hi, sinv_lo)
+    first(schur_copy)
+    convert(c_copy, c_stage, NCZ // c_rows, c_rows, c_hi, c_lo)
+    load_copy.wait()
+    pl.semaphore_wait(barrier, Q + Z)
+    halo_start(0, vld, hs0, hr0)
+
+    row = jnp.zeros((8, LANES), F32)
+    for k in range(SLOTS):
+        row = jnp.where(lane8 == k, cn[k // FACES, k % FACES].astype(F32), row)
+    arb[0] = row
+    q_start(0, arb.at[0], arr.at[0], shared=True)
+
+    for s in range(SUBS):
+        for place, slot in ((s, ups[s]), (SUBS + s, downs[s])):
+            face = jnp.zeros((NCL, E), F32)
+            for f in range(FACES):
+                face = jnp.where(slot == s * FACES + f, basis_t[s, :, f * E:(f + 1) * E], face)
+            bs[place] = face
+    pair_start(4, bs, br, SUBS)
+
     zrow = jnp.zeros((32 - NCL, NI), F32)
     for s in range(SUBS):
         b = basis_t[s]
@@ -226,7 +259,7 @@
     i1 = lax.broadcasted_iota(jnp.int32, sp.shape, 1)
     target = (i0 & 7) * LANES + (i0 >> 7) * 16 + ((i0 & 127) >> 3)
     sp[...] = jnp.where(i1 == target, jnp.float32(1.0), jnp.float32(0.0)).astype(BF16)
-    wide = RR * LANES
+    wide = (RR + 1) * LANES
     j0 = lax.broadcasted_iota(jnp.int32, (CG * LANES, wide), 0)
     j1 = lax.broadcasted_iota(jnp.int32, (CG * LANES, wide), 1)
     back = (j1 & 7) * LANES + (j1 >> 7) * 16 + ((j1 & 127) >> 3)
@@ -239,40 +272,43 @@
     ).astype(BF16)
     xbuf[...] = jnp.zeros_like(xbuf)
 
-    convert(sinv_copy, s_stage, SUBS * NI // s_rows, s_rows, sinv_hi, sinv_lo)
-    first(schur_copy)
-    load_copy.wait()
-    pl.semaphore_wait(barrier, Q + Z)
-    halo_start(0, vld, hs0, hr0)
-
-    row = jnp.zeros((8, LANES), F32)
-    for k in range(SLOTS):
-        row = jnp.where(lane8 == k, cn[k // FACES, k % FACES].astype(F32), row)
-    arb[0] = row
-    q_start(0, arb.at[0], arr.at[0], shared=True)
-
-    convert(c_copy, c_stage, NCZ // c_rows, c_rows, c_hi, c_lo)
-
     settle(0, "in")
     zmine = pl.ds(pl.multiple_of(z * Q, Q), Q)
     arz0[...] = arr[0, pl.ds(0, Q, stride=8), :]
     cnz[zmine, :] = arz0[...]
     z_start(1, lambda t: arz0, cnz.at[zmine, :], cnz.at[pl.ds(0, (Z - 1) * Q), :])
-    convert(schur_copy, s_stage, SUBS * NI // s_rows, s_rows, schur_hi, schur_lo)
-
-    settle(1, "in")
-    cns = cnz[...]
-    cnt = cns.T if ZQ == LANES else jnp.concatenate([cns, jnp.zeros((LANES - ZQ, LANES), F32)], axis=0).T
-    face0 = lax.broadcasted_iota(jnp.int32, (NF, ZQ), 0).astype(F32)
-    face1 = lax.broadcasted_iota(jnp.int32, (ZQ, NFZ), 1).astype(F32) + (z * NFZ).astype(F32)
-    for k in range(SLOTS):
-        scat[:, k * ZQ:(k + 1) * ZQ] = jnp.where(
-            face0 == cnt[k:k + 1, :ZQ], jnp.float32(1.0), jnp.float32(0.0)
-        ).astype(BF16)
-        gath[k] = jnp.where(
-            cns[:, k:k + 1] == face1, jnp.float32(1.0), jnp.float32(0.0)
-        ).astype(BF16)
-
+
+    def number_tables():
+        settle(1, "in")
+        cns = cnz[...]
+        cnt = cns.T if ZQ == LANES else jnp.concatenate([cns, jnp.zeros((LANES - ZQ, LANES), F32)], axis=0).T
+        face0 = lax.broadcasted_iota(jnp.int32, (NF, ZQ), 0).astype(F32)
+        face1 = lax.broadcasted_iota(jnp.int32, (ZQ, NFZ), 1).astype(F32) + (z * NFZ).astype(F32)
+        for k in range(SLOTS):
+            scat[:, k * ZQ:(k + 1) * ZQ] = jnp.where(
+                face0 == cnt[k:k + 1, :ZQ], jnp.float32(1.0), jnp.float32(0.0)
+            ).astype(BF16)
+            gath[k] = jnp.where(
+                cns[:, k:k + 1] == face1, jnp.float32(1.0), jnp.float32(0.0)
+            ).astype(BF16)
+
+    def face_tables():
+        settle(4, 0, "halo in")
+        settle(4, 1, "halo in")
+        pad = jnp.zeros((32 - NCL, E), F32)
+        for c in range(2 * SUBS):
+            b = jnp.concatenate([br[c], pad], axis=0)
+            bh = b.astype(BF16).astype(F32)
+            bface[c] = jnp.concatenate([bh, bh, b - bh, jnp.zeros_like(bh)], axis=0).T.astype(BF16)
+        for s in range(SUBS):
+            for place, slot in ((s, ups[s]), (SUBS + s, downs[s])):
+                local, inside, outside = place_of(slot)
+                b = jnp.concatenate([br[outside], pad], axis=0)
+                bh = b.astype(BF16).astype(F32)
+                both = jnp.concatenate([bh, b - bh], axis=0).astype(BF16)
+                bpart[place] = lax.dot_general(
+                    both, perm[slot][:, :E], (((1,), (1,)), ((), ())), preferred_element_type=F32
+                ).astype(BF16)
 
     def put(k, x):
         hi, lo = split(x)
@@ -280,7 +316,7 @@
         hh[at, :] = hi
         hl[at, :] = lo
 
-    def local_mul(a_hi, a_lo, out):
+    def local_mul(a_hi, a_lo, out, scale):
         rows = 2 * E
         per = NI // rows
 
@@ -290,19 +326,24 @@
             hi = a_hi[at, :]
             top = hh[sub, :]
             acc = dot(hi, top) + dot(hi, hl[sub, :]) + dot(a_lo[at, :], top)
-            out[2 * i] = acc[:E]
-            out[2 * i + 1] = acc[E:]
+            out[2 * i] = scale(2 * i) * acc[:E]
+            out[2 * i + 1] = scale(2 * i + 1) * acc[E:]
             return carry
         lax.fori_loop(0, SUBS * per, body, 0)
 
-    def forward_start(n):
+    def coarse_load(s):
+        sub = pl.ds(s * NI, NI)
+        top = hh[sub, :]
+        x = dot(bt_hi[s], top) + dot(bt_hi[s], hl[sub, :]) + dot(bt_lo[s], top)
+        return x[:NCL]
+
+    def forward_start(n, loads, sums=()):
         for s in range(SUBS):
-            sub = pl.ds(s * NI, NI)
-            top = hh[sub, :]
-            x = dot(bt_hi[s], top) + dot(bt_hi[s], hl[sub, :]) + dot(bt_lo[s], top)
-            xbuf[s * NCL:(s + 1) * NCL, :] = x[:NCL]
+            xbuf[s * NCL:(s + 1) * NCL, :] = loads[s]
+        for i, part in enumerate(sums):
+            xbuf[pl.ds(SUBS * NCL + i, 1), :] = part.sum(axis=0, keepdims=True)
         xt[...] = xbuf[...].T
-        acc = jnp.zeros((2 * Q, wide), F32)
+        acc = jnp.zeros((2 * Q, (RR + 1) * LANES), F32)
         for c in range(CG):
             part = xt[pl.ds(c, Q, stride=CG), :]
             hi = part.astype(BF16).astype(F32)
@@ -310,15 +351,15 @@
             acc += dot(both, spt[c * LANES:(c + 1) * LANES, :])
         acc = acc[:Q] + acc[Q:]
         b = qb.at[n]
-        for r in range(RR):
+        for r in range(RR + 1):
             b[pl.ds(r, Q, stride=8), :] = acc[:, r * LANES:(r + 1) * LANES]
-        for r in range(RR, 8):
+        for r in range(RR + 1, 8):
             b[pl.ds(r, Q, stride=8), :] = jnp.zeros((Q, LANES), F32)
         q_start(2 + 4 * n, b, qr.at[n])
 
     def gather_start(n):
         settle(2 + 4 * n, "in")
-        for r in range(RR):
+        for r in range(RR + 1):
             part = qr[n, pl.ds(r, Q, stride=8), :]
             zb[n, r] = part
             zr[n, r, zmine, :] = part
@@ -327,8 +368,18 @@
             zr.at[n, :, pl.ds(0, (Z - 1) * Q), :],
         )
 
+    def gather_wait(n):
+        settle(3 + 4 * n, "in")
+
+    def own_step(n):
+        tot = jnp.broadcast_to(zr[n, RR].sum(axis=0, keepdims=True), (8, LANES))
+        below = pltpu.roll(tot, LANES - CG, 1)
+        row = jnp.where(lane8 < CG, tot / below, jnp.float32(0.0))
+        for shift in (8, 16, 32, 64):
+            row = row + pltpu.roll(row, shift, 1)
+        return row[0:1]
+
     def coarse_product(n, step=None):
-        settle(3 + 4 * n, "in")
         la = lax.broadcasted_iota(jnp.int32, (ZQ, LANES), 1) >> 5
         pieces = []
         for r in range(RR):
@@ -406,20 +457,31 @@
             yt[pl.ds(c, Q, stride=CG), :] = acc[:Q, cols] + acc[Q:, cols]
         return yt[...].T
 
-    def add_coarse(y):
-        pad = jnp.zeros((32 - NCL, NR), F32)
+    def columns(ys):
+        ys = jnp.concatenate([ys, jnp.zeros((32 - NCL, NR), F32)], axis=0)
+        hi = ys.astype(BF16).astype(F32)
+        return jnp.concatenate([hi, ys - hi, hi, jnp.zeros_like(hi)], axis=0).astype(BF16)
+
+    def add_coarse(n, y, recv):
+        half = SUBS * NCL
+        for way in range(2):
+            ys[n, way] = y[:half]
+        pair_start(6 + n, ys.at[n], yr.at[n], 1)
         for s in range(SUBS):
-            ys = jnp.concatenate([y[s * NCL:(s + 1) * NCL], pad], axis=0)
-            hi = ys.astype(BF16).astype(F32)
-            lo = ys - hi
-            cols = jnp.concatenate([hi, lo, hi, jnp.zeros_like(hi)], axis=0).astype(BF16)
+            cols = columns(y[s * NCL:(s + 1) * NCL])
 
             def body(f, carry):
                 k = s * FACES + f
                 at = pl.ds(pl.multiple_of(f * E, E), E)
-                loc[k] = weight_of(k) * (loc[k] + dot(bcol[s, at, :], cols))
+                loc[k] = loc[k] + weight_of(k) * dot(bcol[s, at, :], cols)
                 return carry
             lax.fori_loop(0, FACES, body, 0)
+        halo_wait(6 + n)
+        halo_wait(1 + 2 * n)
+        for c in range(2 * SUBS):
+            first_row = (c % SUBS) * NCL
+            cols = columns(yr[n, c // SUBS, first_row:first_row + NCL, :])
+            recv[c] = recv[c] + 0.5 * dot(bface[c], cols)
 
     def fold(x):
         return x.reshape(E // 8, 8, NR).sum(axis=0)
@@ -453,15 +515,6 @@
     def cases(tile, i):
         return jnp.concatenate([tile[i * nh + h:i * nh + h + 1, :lw] for h in range(nh)], axis=1)
 
-    def own_cases(tile):
-        row = jnp.where(q * CG >= LANES, tile[nh - 1:nh], tile[0:1])
-        row = jnp.broadcast_to(row, (8, LANES))
-        row = pltpu.roll(row, lax.rem(2 * LANES - q * CG + LANES, LANES), 1)
-        row = jnp.where(lane8 < CG, row, jnp.float32(0.0))
-        for shift in (8, 16, 32, 64):
-            row = row + pltpu.roll(row, shift, 1)
-        return row[0:1]
-
     zero8 = jnp.zeros((8, NR), F32)
 
     halo_wait(0)
@@ -473,14 +526,20 @@
         return carry
     lax.fori_loop(0, SLOTS, residual, 0)
 
-    forward_start(0)
-    local_mul(sinv_hi, sinv_lo, loc)
+    def unscaled(k):
+        return jnp.float32(1.0)
+
+    forward_start(0, [coarse_load(s) for s in range(SUBS)])
+    local_mul(sinv_hi, sinv_lo, loc, weight_of)
     gather_start(0)
+    number_tables()
+    gather_wait(0)
+    halo_start(1, loc, hs1, hr1)
     coarse_product(0)
+    face_tables()
+    convert(schur_copy, s_stage, SUBS * NI // s_rows, s_rows, schur_hi, schur_lo)
     backward_start(0)
-    add_coarse(backward_finish(0))
-    halo_start(1, loc, hs1, hr1)
-    halo_wait(1)
+    add_coarse(0, backward_finish(0), hr1)
 
     def direction(k, acc):
         d = loc[k] + partner(k, loc, hr1)
@@ -489,53 +548,64 @@
         return acc + fold(weight_of(k) * res[k] * d)
     rz_part = lax.fori_loop(0, SLOTS, direction, zero8)
 
-    local_mul(schur_hi, schur_lo, prod)
+    local_mul(schur_hi, schur_lo, prod, unscaled)
+    for s in range(SUBS):
+        for place, slot in ((s, ups[s]), (SUBS + s, downs[s])):
+            hi, lo = split(prod[slot])
+            b = bpart[place]
+            x = dot(b, hi)
+            gs[place] = 0.5 * (x[:NCL] + x[32:32 + NCL] + dot(b[:32], lo)[:NCL])
+    pair_start(5, gs, gr, SUBS)
     halo_start(2, prod, hs2, hr2)
-    halo_wait(2)
-
-    def image(k, acc):
-        m = prod[k] + partner(k, prod, hr2)
-        img[k] = m
-        wm = weight_of(k) * m
-        put(k, wm)
-        return acc + fold(dirn[k] * wm)
-    da_part = lax.fori_loop(0, SLOTS, image, zero8)
-
-    forward_start(1)
+
+    def image_here(k, acc):
+        m = prod[k]
+        put(k, weight_of(k) * (m + partner_here(k, prod)))
+        return acc + fold(dirn[k] * m)
+    da_part = lax.fori_loop(0, SLOTS, image_here, zero8)
+
+    loads = [coarse_load(s) for s in range(SUBS)]
+    halo_wait(5)
+    for s in range(SUBS):
+        loads[s] = loads[s] + gr[place_of(downs[s])[2]] + gr[place_of(ups[s])[2]]
+    forward_start(1, loads, [rz_part, da_part])
     sums_start(0, [rz_part, da_part])
     gather_start(1)
     sums_pass(0)
+    gather_wait(1)
+    coarse_product(1, lambda: own_step(1))
     tot = sums_finish(0)
     rz = cases(tot, 0)
     alpha = rz / cases(tot, 1)
-    coarse_product(1, lambda: own_cases(tot[:nh] / tot[nh:2 * nh]))
+    halo_wait(2)
 
     def advance(k, carry):
-        r = res[k] - alpha * img[k]
-        res[k] = r
+        m = prod[k] + partner(k, prod, hr2)
+        img[k] = m
+        r = res[k] - alpha * m
+        vld[k] = r
         put(k, weight_of(k) * r)
         return carry
     lax.fori_loop(0, SLOTS, advance, 0)
 
-    local_mul(sinv_hi, sinv_lo, loc)
+    local_mul(sinv_hi, sinv_lo, loc, weight_of)
     backward_start(1)
+    halo_start(3, loc, hs3, hr3)
 
     def energies(k, acc):
-        return acc + fold(weight_of(k) * res[k] * loc[k])
+        return acc + fold(vld[k] * loc[k])
     sums_start(1, [lax.fori_loop(0, SLOTS, energies, zero8)])
     y = backward_finish(1)
     coarse_energy = y[SUBS * NCL:SUBS * NCL + NCF].sum(axis=0, keepdims=True)
-    add_coarse(y)
-    halo_start(3, loc, hs3, hr3)
     sums_pass(1)
-    beta = (cases(sums_finish(1), 0) + coarse_energy) / rz
-    halo_wait(3)
+    add_coarse(1, y, hr3)
 
     def second(k, carry):
         pre[k] = loc[k] + partner(k, loc, hr3)
         return carry
     lax.fori_loop(0, SLOTS, second, 0)
-    out_ab[...] = jnp.concatenate([alpha, beta, jnp.zeros((6, NR), F32)], axis=0)
+    out_alpha[...] = alpha
+    out_beta[...] = (cases(sums_finish(1), 0) + coarse_energy) / rz
 
     for wait in list(owed.values()):
         wait()
@@ -552,15 +622,17 @@
     halo = pltpu.VMEM((2 * SUBS, E, NR), F32)
     mat = pltpu.VMEM((SUBS * NI, NI), BF16)
     out = pltpu.VMEM((SLOTS, E, NR), F32)
+    ratio = pltpu.VMEM((1, NR), F32)
+    NCL = FACES * NCF
     anywhere = pl.BlockSpec(memory_space=pl.ANY)
     vmem = pl.BlockSpec(memory_space=pltpu.VMEM)
     smem = pl.BlockSpec(memory_space=pltpu.SMEM)
-    direction, residual, preconditioned, ratios = pl.pallas_call(
+    direction, residual, image, preconditioned, alpha, beta = pl.pallas_call(
         functools.partial(kernel, Q, Z),
-        out_shape=(out, out, out, jax.ShapeDtypeStruct((8, NR), F32)),
+        out_shape=(out, out, out, out, ratio, ratio),
         in_specs=[anywhere, anywhere, anywhere, vmem, anywhere, smem, vmem, smem],
-        out_specs=(vmem, vmem, vmem, vmem),
-        scratch_shapes=[vec] * 4 + [halo] * 8 + [mat] * 4 + [
+        out_specs=(vmem,) * 6,
+        scratch_shapes=[vec] * 3 + [halo] * 8 + [mat] * 4 + [
             pltpu.VMEM((NCZ, NC0), BF16),
             pltpu.VMEM((NCZ, NC0), BF16),
             pltpu.VMEM((2, 2 * E, NI), F32),
@@ -571,8 +643,16 @@
             pltpu.VMEM((SUBS, 32, NI), BF16),
             pltpu.VMEM((SUBS, 32, NI), BF16),
             pltpu.VMEM((SUBS, NI, LANES), BF16),
+            pltpu.VMEM((2 * SUBS, E, LANES), BF16),
+            pltpu.VMEM((2 * SUBS, 64, E), BF16),
+            pltpu.VMEM((2 * SUBS, NCL, E), F32),
+            pltpu.VMEM((2 * SUBS, NCL, E), F32),
+            pltpu.VMEM((2 * SUBS, NCL, NR), F32),
+            pltpu.VMEM((2 * SUBS, NCL, NR), F32),
+            pltpu.VMEM((2, 2, SUBS * NCL, NR), F32),
+            pltpu.VMEM((2, 2, SUBS * NCL, NR), F32),
             pltpu.VMEM(((RR + 1) * LANES, CG * LANES), BF16),
-            pltpu.VMEM((CG * LANES, RR * LANES), BF16),
+            pltpu.VMEM((CG * LANES, (RR + 1) * LANES), BF16),
             pltpu.VMEM((2 * NCF * LANES, LANES), BF16),
             pltpu.VMEM((NF, SLOTS * ZQ), BF16),
             pltpu.VMEM((SLOTS, ZQ, NF // Z), BF16),
@@ -585,8 +665,8 @@
             pltpu.VMEM((NCZ, LANES), F32),
             pltpu.VMEM((4, Q * 8, LANES), F32),
             pltpu.VMEM((4, Q * 8, LANES), F32),
-            pltpu.VMEM((2, RR, Q, LANES), F32),
-            pltpu.VMEM((2, RR, ZQ, LANES), F32),
+            pltpu.VMEM((2, RR + 1, Q, LANES), F32),
+            pltpu.VMEM((2, RR + 1, ZQ, LANES), F32),
             pltpu.VMEM((2, RR + 1, ZQ, LANES), F32),
             pltpu.VMEM((Z, RR + 1, Q, LANES), F32),
             pltpu.VMEM((Z, RR + 1, Q, LANES), F32),
@@ -600,8 +680,8 @@
             pltpu.SemaphoreType.DMA((2,)),
             pltpu.SemaphoreType.DMA((14,)),
             pltpu.SemaphoreType.DMA((14,)),
-            pltpu.SemaphoreType.DMA((4, 2)),
-            pltpu.SemaphoreType.DMA((4, 2)),
+            pltpu.SemaphoreType.DMA((8, 2)),
+            pltpu.SemaphoreType.DMA((8, 2)),
         ],
         compiler_params=pltpu.CompilerParams(
             collective_id=0, has_side_effects=True, vmem_limit_bytes=56 * 1024 * 1024
@@ -616,10 +696,9 @@
         jnp.swapaxes(edge_map, 0, 1),
         coarse_number,
     )
-    alpha, beta = ratios[0], ratios[1]
     return tuple(
         o.reshape(load.shape)
-        for o in (alpha * direction, residual, preconditioned + beta * direction)
+        for o in (alpha * direction, residual - alpha * image, preconditioned + beta * direction)
     )
 
 

time: 128 us -> 115 us (0.90)
  Pallas kernels: 123 us -> 112 us
  local copies, waits for them, and re-layouts: 1.92 us -> 0 us
    pallas_call x1, Pallas kernels: 123 us -> 112 us  [shards(): pl.pallas_call(functools.partial(kernel, Q, Z), out_shape=(out, out, out,...]
where the time goes in v3:
time: 115 us
  Pallas kernels  112 us (97%)
  other arithmetic  2.35 us (2%)
    pallas_call x1, Pallas kernels, shards(): pl.pallas_call(functools.partial(kernel, Q, Z), out_shape=(out, out, out,...  112 us
    add x1, other arithmetic, shards(): preconditioned + beta * direction  2.35 us

profile of v3, /device:TPU:1, one launch (start us, length us, event | category | flops | bytes accessed | tf_op | source)
XLA Modules:
  0.0 115.1 jit_solution(5857872310618723923)
XLA Ops:
  0.6 112.1 %shard_map.103 = (f32[12,128,256]{2,1,0:T(8,128)S(1)}, f32[12,128,256]{2,1,0:T(8,128)S(1)}, f32[12,128,256]{2,1,0:T(8,128)S(1)}, f32[12,128,256]{2,1,0:T(8,128)S...) custom-call(f32[12,128,256]{2,1,0:T(8,128)} %bitcast.14, f32[1536,768]{1,0:T(8,128)} %bitcast.12, f32[1536,768]{1,0:T(8,128)} %bitcast.13, ...), custom_call_target="tpu_custom_call" | custom-call | tf_op jit(solution)/shard_map/pallas_call | solution.py:630
  112.7 2.3 %multiply_add_fusion = (f32[12,128,256]{2,1,0:T(8,128)}, f32[12,128,256]{2,1,0:T(8,128)}, f32[12,128,256]{2,1,0:T(8,128)}) fusion(f32[12,128,256]{2,1,0:T(8,128)S(1)} %get-tuple-element.13, f32[12,128,256]{2,1,0:T(8,128)S(1)} %get-tuple-element.10, f32[256]{0:T(256)S(1)} %bitcast.11, f32[256]{0:T(256)S(1)} %bitcast.10, ...), kind=kLoop, calls=%fused_computation | loop fusion | flops 1966080 | bytes 11012096 | tf_op jit(solution)/shard_map/add | solution.py:701

commit v4 on v3

--- a/solution.py
+++ b/solution.py
@@ -2,6 +2,7 @@
 
 import jax
 import jax.numpy as jnp
+import numpy as np
 from jax import lax
 from jax.experimental import pallas as pl
 from jax.experimental.pallas import tpu as pltpu
@@ -28,7 +29,7 @@
 
 
 def kernel(
-    Q, Z, load, schur, sinv, basis_t, coarse, ps, em, cn,
+    Q, Z, load, schur, sinv, basis_t, coarse, ps, em, cn, sp_in, spt_in, fold4_in,
     dirn, res, img, pre, out_alpha, out_beta,
     vld, loc, prod,
     hs0, hs1, hs2, hs3, hr0, hr1, hr2, hr3,
@@ -36,7 +37,7 @@
     hh, hl, perm, bt_hi, bt_lo, bcol, bface, bpart, bs, br, gs, gr, ys, yr, sp, spt,
     fold4, scat, gath, xbuf, xt, yt, xm, xb, xf0, y2,
     qb, qr, zb, zr, ob, zs0, zs1, arb, arr, arz0, arz1, cnz,
-    in_sem, st_sem, ct_sem, q_send, q_recv, h_send, h_recv,
+    in_sem, tab_sem, st_sem, ct_sem, q_send, q_recv, h_send, h_recv,
 ):
     q = lax.axis_index("sub")
     z = lax.axis_index("coarse")
@@ -108,6 +109,12 @@
 
     first(sinv_copy)
     first(c_copy)
+    tables = [
+        pltpu.make_async_copy(src, dst, tab_sem.at[i])
+        for i, (src, dst) in enumerate(((sp_in, sp), (spt_in, spt), (fold4_in, fold4)))
+    ]
+    for copy in tables:
+        copy.start()
 
     barrier = pltpu.get_barrier_semaphore()
 
@@ -190,6 +197,19 @@
             send[SUBS + s] = v[downs[s]]
         pair_start(h, send, recv, SUBS)
 
+    def half_start(h, s, v, send, recv):
+        for way, slot, device in ((0, ups[s], nxt_id), (1, downs[s], prv_id)):
+            place = way * SUBS + s
+            send[place] = v[slot]
+            part = pl.ds(place, 1)
+            pltpu.make_async_remote_copy(
+                src_ref=send.at[part], dst_ref=recv.at[part],
+                send_sem=h_send.at[h, way], recv_sem=h_recv.at[h, way],
+                device_id=device, device_id_type=MESH,
+            ).start()
+            owe((h, way, "halo in"), recv.at[part], h_recv.at[h, way])
+            owe((h, way, "halo out"), recv.at[part], h_send.at[h, way])
+
     def halo_wait(h):
         settle(h, 0, "halo in")
         settle(h, 1, "halo in")
@@ -225,7 +245,6 @@
     NCL = FACES * NCF
     convert(sinv_copy, s_stage, SUBS * NI // s_rows, s_rows, sinv_hi, sinv_lo)
     first(schur_copy)
-    convert(c_copy, c_stage, NCZ // c_rows, c_rows, c_hi, c_lo)
     load_copy.wait()
     pl.semaphore_wait(barrier, Q + Z)
     halo_start(0, vld, hs0, hr0)
@@ -255,22 +274,11 @@
         bt_lo[s] = bl.astype(BF16)
         bcol[s] = jnp.concatenate([bh, bh, bl, jnp.zeros_like(bl)], axis=0).T.astype(BF16)
 
-    i0 = lax.broadcasted_iota(jnp.int32, sp.shape, 0)
-    i1 = lax.broadcasted_iota(jnp.int32, sp.shape, 1)
-    target = (i0 & 7) * LANES + (i0 >> 7) * 16 + ((i0 & 127) >> 3)
-    sp[...] = jnp.where(i1 == target, jnp.float32(1.0), jnp.float32(0.0)).astype(BF16)
-    wide = (RR + 1) * LANES
-    j0 = lax.broadcasted_iota(jnp.int32, (CG * LANES, wide), 0)
-    j1 = lax.broadcasted_iota(jnp.int32, (CG * LANES, wide), 1)
-    back = (j1 & 7) * LANES + (j1 >> 7) * 16 + ((j1 & 127) >> 3)
-    spt[...] = jnp.where(j0 == back, jnp.float32(1.0), jnp.float32(0.0)).astype(BF16)
-
-    m0 = lax.broadcasted_iota(jnp.int32, fold4.shape, 0)
-    m1 = lax.broadcasted_iota(jnp.int32, fold4.shape, 1)
-    fold4[...] = jnp.where(
-        ((m0 & 7) == (m1 & 7)) & ((m0 >> 8) == ((m1 >> 3) & 3)), jnp.float32(1.0), jnp.float32(0.0)
-    ).astype(BF16)
     xbuf[...] = jnp.zeros_like(xbuf)
+
+    convert(c_copy, c_stage, NCZ // c_rows, c_rows, c_hi, c_lo)
+    for copy in tables:
+        copy.wait()
 
     settle(0, "in")
     zmine = pl.ds(pl.multiple_of(z * Q, Q), Q)
@@ -316,7 +324,7 @@
         hh[at, :] = hi
         hl[at, :] = lo
 
-    def local_mul(a_hi, a_lo, out, scale):
+    def local_mul(a_hi, a_lo, out, scale, subs=range(SUBS)):
         rows = 2 * E
         per = NI // rows
 
@@ -329,7 +337,7 @@
             out[2 * i] = scale(2 * i) * acc[:E]
             out[2 * i + 1] = scale(2 * i + 1) * acc[E:]
             return carry
-        lax.fori_loop(0, SUBS * per, body, 0)
+        lax.fori_loop(subs[0] * per, (subs[-1] + 1) * per, body, 0)
 
     def coarse_load(s):
         sub = pl.ds(s * NI, NI)
@@ -462,11 +470,12 @@
         hi = ys.astype(BF16).astype(F32)
         return jnp.concatenate([hi, ys - hi, hi, jnp.zeros_like(hi)], axis=0).astype(BF16)
 
+    def share_coarse(n, y):
+        for way in range(2):
+            ys[n, way] = y[:SUBS * NCL]
+        pair_start(6 + n, ys.at[n], yr.at[n], 1)
+
     def add_coarse(n, y, recv):
-        half = SUBS * NCL
-        for way in range(2):
-            ys[n, way] = y[:half]
-        pair_start(6 + n, ys.at[n], yr.at[n], 1)
         for s in range(SUBS):
             cols = columns(y[s * NCL:(s + 1) * NCL])
 
@@ -478,6 +487,7 @@
             lax.fori_loop(0, FACES, body, 0)
         halo_wait(6 + n)
         halo_wait(1 + 2 * n)
+        halo_wait(8 + n)
         for c in range(2 * SUBS):
             first_row = (c % SUBS) * NCL
             cols = columns(yr[n, c // SUBS, first_row:first_row + NCL, :])
@@ -530,16 +540,20 @@
         return jnp.float32(1.0)
 
     forward_start(0, [coarse_load(s) for s in range(SUBS)])
-    local_mul(sinv_hi, sinv_lo, loc, weight_of)
+    local_mul(sinv_hi, sinv_lo, loc, weight_of, (0,))
+    half_start(1, 0, loc, hs1, hr1)
+    local_mul(sinv_hi, sinv_lo, loc, weight_of, (1,))
     gather_start(0)
     number_tables()
     gather_wait(0)
-    halo_start(1, loc, hs1, hr1)
+    half_start(8, 1, loc, hs1, hr1)
     coarse_product(0)
     face_tables()
     convert(schur_copy, s_stage, SUBS * NI // s_rows, s_rows, schur_hi, schur_lo)
     backward_start(0)
-    add_coarse(0, backward_finish(0), hr1)
+    y = backward_finish(0)
+    share_coarse(0, y)
+    add_coarse(0, y, hr1)
 
     def direction(k, acc):
         d = loc[k] + partner(k, loc, hr1)
@@ -588,14 +602,17 @@
         return carry
     lax.fori_loop(0, SLOTS, advance, 0)
 
-    local_mul(sinv_hi, sinv_lo, loc, weight_of)
+    local_mul(sinv_hi, sinv_lo, loc, weight_of, (0,))
+    half_start(3, 0, loc, hs3, hr3)
+    local_mul(sinv_hi, sinv_lo, loc, weight_of, (1,))
     backward_start(1)
-    halo_start(3, loc, hs3, hr3)
+    half_start(9, 1, loc, hs3, hr3)
 
     def energies(k, acc):
         return acc + fold(vld[k] * loc[k])
     sums_start(1, [lax.fori_loop(0, SLOTS, energies, zero8)])
     y = backward_finish(1)
+    share_coarse(1, y)
     coarse_energy = y[SUBS * NCL:SUBS * NCL + NCF].sum(axis=0, keepdims=True)
     sums_pass(1)
     add_coarse(1, y, hr3)
@@ -609,6 +626,17 @@
 
     for wait in list(owed.values()):
         wait()
+
+
+def one_hot_tables():
+    rows = (SLOTS * NCF * CG // LANES + 1) * LANES
+    i0 = np.arange(rows)[:, None]
+    i1 = np.arange(CG * LANES)[None, :]
+    table = i1 == (i0 % CG) * LANES + (i0 // LANES) * (LANES // CG) + i0 % LANES // CG
+    m0 = np.arange(2 * NCF * LANES)[:, None]
+    m1 = np.arange(LANES)[None, :]
+    fold = (m0 % CG == m1 % CG) & (m0 // (2 * LANES) == m1 // CG % NCF)
+    return [jnp.asarray(t.astype(np.float32), BF16) for t in (table, table.T, fold)]
 
 
 def shards(Q, Z, load, schur, schur_inverse, basis, coarse_inverse, partner_slot, edge_map, coarse_number):
@@ -630,7 +658,7 @@
     direction, residual, image, preconditioned, alpha, beta = pl.pallas_call(
         functools.partial(kernel, Q, Z),
         out_shape=(out, out, out, out, ratio, ratio),
-        in_specs=[anywhere, anywhere, anywhere, vmem, anywhere, smem, vmem, smem],
+        in_specs=[anywhere, anywhere, anywhere, vmem, anywhere, smem, vmem, smem] + [anywhere] * 3,
         out_specs=(vmem,) * 6,
         scratch_shapes=[vec] * 3 + [halo] * 8 + [mat] * 4 + [
             pltpu.VMEM((NCZ, NC0), BF16),
@@ -676,12 +704,13 @@
             pltpu.VMEM((2, Z, 8, LANES), F32),
             pltpu.VMEM((ZQ, LANES), F32),
             pltpu.SemaphoreType.DMA,
+            pltpu.SemaphoreType.DMA((3,)),
             pltpu.SemaphoreType.DMA((2,)),
             pltpu.SemaphoreType.DMA((2,)),
             pltpu.SemaphoreType.DMA((14,)),
             pltpu.SemaphoreType.DMA((14,)),
-            pltpu.SemaphoreType.DMA((8, 2)),
-            pltpu.SemaphoreType.DMA((8, 2)),
+            pltpu.SemaphoreType.DMA((10, 2)),
+            pltpu.SemaphoreType.DMA((10, 2)),
         ],
         compiler_params=pltpu.CompilerParams(
             collective_id=0, has_side_effects=True, vmem_limit_bytes=56 * 1024 * 1024
@@ -695,6 +724,7 @@
         partner_slot,
         jnp.swapaxes(edge_map, 0, 1),
         coarse_number,
+        *one_hot_tables(),
     )
     return tuple(
         o.reshape(load.shape)

time: 115 us -> 108 us (0.939)
  Pallas kernels: 112 us -> 105 us
    pallas_call x1, Pallas kernels: 112 us -> 105 us  [shards(): pl.pallas_call(functools.partial(kernel, Q, Z), out_shape=(out, out, out,...]
where the time goes in v4:
time: 108 us
  Pallas kernels  105 us (97%)
  other arithmetic  2.35 us (2%)
    pallas_call x1, Pallas kernels, shards(): pl.pallas_call(functools.partial(kernel, Q, Z), out_shape=(out, out, out,...  105 us
    add x1, other arithmetic, shards(): preconditioned + beta * direction  2.35 us

profile of v4, /device:TPU:1, one launch (start us, length us, event | category | flops | bytes accessed | tf_op | source)
XLA Modules:
  0.0 107.7 jit_solution(1468443155391154298)
XLA Ops:
  0.6 104.7 %shard_map.130 = (f32[12,128,256]{2,1,0:T(8,128)S(1)}, f32[12,128,256]{2,1,0:T(8,128)S(1)}, f32[12,128,256]{2,1,0:T(8,128)S(1)}, f32[12,128,256]{2,1,0:T(8,128)S...) custom-call(f32[12,128,256]{2,1,0:T(8,128)} %bitcast.17, f32[1536,768]{1,0:T(8,128)} %bitcast.12, f32[1536,768]{1,0:T(8,128)} %bitcast.13, ...), custom_call_target="tpu_custom_call" | custom-call | tf_op jit(solution)/shard_map/pallas_call | solution.py:658
  105.3 2.3 %multiply_add_fusion = (f32[12,128,256]{2,1,0:T(8,128)}, f32[12,128,256]{2,1,0:T(8,128)}, f32[12,128,256]{2,1,0:T(8,128)}) fusion(f32[12,128,256]{2,1,0:T(8,128)S(1)} %get-tuple-element.13, f32[12,128,256]{2,1,0:T(8,128)S(1)} %get-tuple-element.10, f32[256]{0:T(256)S(1)} %bitcast.11, f32[256]{0:T(256)S(1)} %bitcast.10, ...), kind=kLoop, calls=%fused_computation | loop fusion | flops 1966080 | bytes 11012096 | tf_op jit(solution)/shard_map/add | solution.py:731

commit v5 on v4

--- a/solution.py
+++ b/solution.py
@@ -16,6 +16,8 @@
 SLOTS = FACES * SUBS
 NCF = 4
 LANES = 128
+STEP = 4
+USED = 4
 CG = 8
 
 
@@ -132,18 +134,18 @@
     def q_start(ph, src, dst, shared=False):
         def body(i, carry):
             p = q_peer(1 + lax.rem(i + Q // 2 - 1, Q - 1))
-            block = src if shared else src.at[pl.ds(pl.multiple_of(p * 8, 8), 8), :]
+            block = src.at[pl.ds(0 if shared else pl.multiple_of(p * 8, 8), USED), :]
             pltpu.make_async_remote_copy(
                 src_ref=block,
-                dst_ref=dst.at[pl.ds(pl.multiple_of(q * 8, 8), 8), :],
+                dst_ref=dst.at[pl.ds(pl.multiple_of(q * 8, 8), USED), :],
                 send_sem=q_send.at[ph], recv_sem=q_recv.at[ph],
                 device_id=(p, z), device_id_type=MESH,
             ).start()
             return carry
         lax.fori_loop(0, Q - 1, body, 0)
-        mine = pl.ds(pl.multiple_of(q * 8, 8), 8)
-        dst[mine, :] = src[...] if shared else src[mine, :]
-        every = dst.at[pl.ds(0, (Q - 1) * 8), :]
+        mine = pl.ds(pl.multiple_of(q * 8, 8), USED)
+        dst[mine, :] = src[0:USED, :] if shared else src[mine, :]
+        every = dst.at[pl.ds(0, (Q - 1) * USED), :]
         owe((ph, "in"), every, q_recv.at[ph])
         owe((ph, "out"), every, q_send.at[ph])
 
@@ -325,19 +327,15 @@
         hl[at, :] = lo
 
     def local_mul(a_hi, a_lo, out, scale, subs=range(SUBS)):
-        rows = 2 * E
-        per = NI // rows
-
-        def body(i, carry):
-            at = pl.ds(pl.multiple_of(i * rows, rows), rows)
-            sub = pl.ds(pl.multiple_of((i // per) * NI, NI), NI)
-            hi = a_hi[at, :]
-            top = hh[sub, :]
-            acc = dot(hi, top) + dot(hi, hl[sub, :]) + dot(a_lo[at, :], top)
-            out[2 * i] = scale(2 * i) * acc[:E]
-            out[2 * i + 1] = scale(2 * i + 1) * acc[E:]
+        def body(s, carry):
+            at = pl.ds(pl.multiple_of(s * NI, NI), NI)
+            top = hh[at, :]
+            acc = dot(a_hi[at, :], top) + dot(a_hi[at, :], hl[at, :]) + dot(a_lo[at, :], top)
+            for f in range(FACES):
+                k = s * FACES + f
+                out[k] = scale(k) * acc[f * E:(f + 1) * E]
             return carry
-        lax.fori_loop(subs[0] * per, (subs[-1] + 1) * per, body, 0)
+        lax.fori_loop(subs[0], subs[-1] + 1, body, 0)
 
     def coarse_load(s):
         sub = pl.ds(s * NI, NI)
@@ -361,19 +359,18 @@
         b = qb.at[n]
         for r in range(RR + 1):
             b[pl.ds(r, Q, stride=8), :] = acc[:, r * LANES:(r + 1) * LANES]
-        for r in range(RR + 1, 8):
-            b[pl.ds(r, Q, stride=8), :] = jnp.zeros((Q, LANES), F32)
         q_start(2 + 4 * n, b, qr.at[n])
 
     def gather_start(n):
         settle(2 + 4 * n, "in")
-        for r in range(RR + 1):
+        for r in range(RR + n):
             part = qr[n, pl.ds(r, Q, stride=8), :]
             zb[n, r] = part
             zr[n, r, zmine, :] = part
+        used = pl.ds(0, RR + n)
         z_start(
-            3 + 4 * n, lambda t: zb.at[n], zr.at[n, :, zmine, :],
-            zr.at[n, :, pl.ds(0, (Z - 1) * Q), :],
+            3 + 4 * n, lambda t: zb.at[n, used], zr.at[n, used, zmine, :],
+            zr.at[n, used, pl.ds(0, (Z - 1) * Q), :],
         )
 
     def gather_wait(n):
@@ -427,35 +424,37 @@
                 g = dot(gath[NCF * r + a], both)
                 o = jnp.where(la == a, g[:, :LANES] + g[:, LANES:], o)
             ob[n, r] = o
-        mine = xf0[pl.ds(pl.multiple_of(z * NFZ, 8) if NFZ % 8 == 0 else z * NFZ, NFZ), :]
-        energy = (mine * y).sum(axis=0, keepdims=True)
-        ob[n, RR] = jnp.where(la == 0, energy, jnp.float32(0.0))
+        if n == 1:
+            mine = xf0[pl.ds(pl.multiple_of(z * NFZ, 8) if NFZ % 8 == 0 else z * NFZ, NFZ), :]
+            energy = (mine * y).sum(axis=0, keepdims=True)
+            ob[n, RR] = jnp.where(la == 0, energy, jnp.float32(0.0))
+        used = pl.ds(0, RR + n)
         zs = (zs0, zs1)[n]
-        zs[z] = ob[n, :, zmine, :]
+        zs[z, used] = ob[n, used, zmine, :]
         z_start(
             4 + 4 * n,
-            lambda t: ob.at[n, :, pl.ds(pl.multiple_of(t * Q, Q), Q), :],
-            zs.at[z],
-            zs.at[pl.ds(0, Z - 1)],
+            lambda t: ob.at[n, used, pl.ds(pl.multiple_of(t * Q, Q), Q), :],
+            zs.at[z, used],
+            zs.at[pl.ds(0, Z - 1), used],
         )
 
     def backward_start(n):
         zs = (zs0, zs1)[n]
         settle(4 + 4 * n, "in")
         b = qb.at[2 + n]
-        for r in range(RR + 1):
+        for r in range(RR + n):
             tot = zs[0, r]
             for t in range(1, Z):
                 tot = tot + zs[t, r]
             b[pl.ds(r, Q, stride=8), :] = tot
-        for r in range(RR + 1, 8):
+        for r in range(RR + n, RR + 1):
             b[pl.ds(r, Q, stride=8), :] = jnp.zeros((Q, LANES), F32)
         q_start(5 + 4 * n, b, qr.at[2 + n])
 
     def backward_finish(n):
         settle(5 + 4 * n, "in")
         acc = jnp.zeros((2 * Q, CG * LANES), F32)
-        for r in range(RR + 1):
+        for r in range(RR + n):
             part = qr[2 + n, pl.ds(r, Q, stride=8), :]
             hi = part.astype(BF16).astype(F32)
             both = jnp.concatenate([hi, part - hi], axis=0).astype(BF16)
@@ -479,12 +478,14 @@
         for s in range(SUBS):
             cols = columns(y[s * NCL:(s + 1) * NCL])
 
-            def body(f, carry):
-                k = s * FACES + f
-                at = pl.ds(pl.multiple_of(f * E, E), E)
-                loc[k] = loc[k] + weight_of(k) * dot(bcol[s, at, :], cols)
+            def body(i, carry):
+                for j in range(3):
+                    f = 3 * i + j
+                    k = s * FACES + f
+                    at = pl.ds(pl.multiple_of(f * E, E), E)
+                    loc[k] = loc[k] + weight_of(k) * dot(bcol[s, at, :], cols)
                 return carry
-            lax.fori_loop(0, FACES, body, 0)
+            lax.fori_loop(0, FACES // 3, body, 0)
         halo_wait(6 + n)
         halo_wait(1 + 2 * n)
         halo_wait(8 + n)
@@ -511,6 +512,7 @@
     def sums_pass(n):
         settle(10 + 2 * n, "in")
         tot = arr[1 + n].reshape(Q, 8, LANES).sum(axis=0)
+        tot = jnp.where(lax.broadcasted_iota(jnp.int32, (8, LANES), 0) < USED, tot, jnp.float32(0.0))
         arb[3 + n] = tot
         arz1[n, z] = tot
         z_start(11 + 2 * n, lambda t: arb.at[3 + n], arz1.at[n, z], arz1.at[n, pl.ds(0, Z - 1)])
@@ -525,6 +527,13 @@
     def cases(tile, i):
         return jnp.concatenate([tile[i * nh + h:i * nh + h + 1, :lw] for h in range(nh)], axis=1)
 
+    def over_slots(body, carry):
+        def some(i, carry):
+            for k in range(STEP):
+                carry = body(STEP * i + k, carry)
+            return carry
+        return lax.fori_loop(0, SLOTS // STEP, some, carry)
+
     zero8 = jnp.zeros((8, NR), F32)
 
     halo_wait(0)
@@ -534,7 +543,7 @@
         res[k] = r
         put(k, weight_of(k) * r)
         return carry
-    lax.fori_loop(0, SLOTS, residual, 0)
+    over_slots(residual, 0)
 
     def unscaled(k):
         return jnp.float32(1.0)
@@ -560,7 +569,7 @@
         dirn[k] = d
         put(k, d)
         return acc + fold(weight_of(k) * res[k] * d)
-    rz_part = lax.fori_loop(0, SLOTS, direction, zero8)
+    rz_part = over_slots(direction, zero8)
 
     local_mul(schur_hi, schur_lo, prod, unscaled)
     for s in range(SUBS):
@@ -576,7 +585,7 @@
         m = prod[k]
         put(k, weight_of(k) * (m + partner_here(k, prod)))
         return acc + fold(dirn[k] * m)
-    da_part = lax.fori_loop(0, SLOTS, image_here, zero8)
+    da_part = over_slots(image_here, zero8)
 
     loads = [coarse_load(s) for s in range(SUBS)]
     halo_wait(5)
@@ -600,7 +609,7 @@
         vld[k] = r
         put(k, weight_of(k) * r)
         return carry
-    lax.fori_loop(0, SLOTS, advance, 0)
+    over_slots(advance, 0)
 
     local_mul(sinv_hi, sinv_lo, loc, weight_of, (0,))
     half_start(3, 0, loc, hs3, hr3)
@@ -610,7 +619,7 @@
 
     def energies(k, acc):
         return acc + fold(vld[k] * loc[k])
-    sums_start(1, [lax.fori_loop(0, SLOTS, energies, zero8)])
+    sums_start(1, [over_slots(energies, zero8)])
     y = backward_finish(1)
     share_coarse(1, y)
     coarse_energy = y[SUBS * NCL:SUBS * NCL + NCF].sum(axis=0, keepdims=True)
@@ -620,7 +629,7 @@
     def second(k, carry):
         pre[k] = loc[k] + partner(k, loc, hr3)
         return carry
-    lax.fori_loop(0, SLOTS, second, 0)
+    over_slots(second, 0)
     out_alpha[...] = alpha
     out_beta[...] = (cases(sums_finish(1), 0) + coarse_energy) / rz
 

time: 108 us -> 99.7 us (0.923)
  Pallas kernels: 105 us -> 96.4 us
    pallas_call x1, Pallas kernels: 105 us -> 96.4 us  [shards(): pl.pallas_call(functools.partial(kernel, Q, Z), out_shape=(out, out, out,...]
where the time goes in v5:
time: 99.7 us; the launch traced here: 99.4 us
  Pallas kernels  96.4 us (97%)
  other arithmetic  2.35 us (2%)
    pallas_call x1, Pallas kernels, shards(): pl.pallas_call(functools.partial(kernel, Q, Z), out_shape=(out, out, out,...  96.4 us
    add x1, other arithmetic, shards(): preconditioned + beta * direction  2.35 us

profile of v5, /device:TPU:1, one launch (start us, length us, event | category | flops | bytes accessed | tf_op | source)
XLA Modules:
  0.0 99.4 jit_solution(5115141258588886289)
XLA Ops:
  0.6 96.4 %shard_map.130 = (f32[12,128,256]{2,1,0:T(8,128)S(1)}, f32[12,128,256]{2,1,0:T(8,128)S(1)}, f32[12,128,256]{2,1,0:T(8,128)S(1)}, f32[12,128,256]{2,1,0:T(8,128)S...) custom-call(f32[12,128,256]{2,1,0:T(8,128)} %bitcast.17, f32[1536,768]{1,0:T(8,128)} %bitcast.12, f32[1536,768]{1,0:T(8,128)} %bitcast.13, ...), custom_call_target="tpu_custom_call" | custom-call | tf_op jit(solution)/shard_map/pallas_call | solution.py:667
  97.1 2.3 %multiply_add_fusion = (f32[12,128,256]{2,1,0:T(8,128)}, f32[12,128,256]{2,1,0:T(8,128)}, f32[12,128,256]{2,1,0:T(8,128)}) fusion(f32[12,128,256]{2,1,0:T(8,128)S(1)} %get-tuple-element.13, f32[12,128,256]{2,1,0:T(8,128)S(1)} %get-tuple-element.10, f32[256]{0:T(256)S(1)} %bitcast.11, f32[256]{0:T(256)S(1)} %bitcast.10, ...), kind=kLoop, calls=%fused_computation | loop fusion | flops 1966080 | bytes 11012096 | tf_op jit(solution)/shard_map/add | solution.py:740

commit v6 on v5

--- a/solution.py
+++ b/solution.py
@@ -16,7 +16,7 @@
 SLOTS = FACES * SUBS
 NCF = 4
 LANES = 128
-STEP = 4
+STEP = 6
 USED = 4
 CG = 8
 
@@ -39,7 +39,7 @@
     hh, hl, perm, bt_hi, bt_lo, bcol, bface, bpart, bs, br, gs, gr, ys, yr, sp, spt,
     fold4, scat, gath, xbuf, xt, yt, xm, xb, xf0, y2,
     qb, qr, zb, zr, ob, zs0, zs1, arb, arr, arz0, arz1, cnz,
-    in_sem, tab_sem, st_sem, ct_sem, q_send, q_recv, h_send, h_recv,
+    in_sem, tab_sem, st_sem, ct_sem, q_send, q_recv, h_send, h_recv, eb, er,
 ):
     q = lax.axis_index("sub")
     z = lax.axis_index("coarse")
@@ -131,9 +131,13 @@
 
     lane8 = lax.broadcasted_iota(jnp.int32, (8, LANES), 1)
 
+    def far(k):
+        x, y = k // 8, k // 2 % 4
+        return min(x, 4 - x) + min(y, 4 - y)
+
     def q_start(ph, src, dst, shared=False):
-        def body(i, carry):
-            p = q_peer(1 + lax.rem(i + Q // 2 - 1, Q - 1))
+        def body(k, carry):
+            p = q_peer(k)
             block = src.at[pl.ds(0 if shared else pl.multiple_of(p * 8, 8), USED), :]
             pltpu.make_async_remote_copy(
                 src_ref=block,
@@ -142,7 +146,11 @@
                 device_id=(p, z), device_id_type=MESH,
             ).start()
             return carry
-        lax.fori_loop(0, Q - 1, body, 0)
+        if shared:
+            lax.fori_loop(1, Q, body, 0)
+        else:
+            for k in sorted(range(1, Q), key=lambda k: -far(k)):
+                body(k, 0)
         mine = pl.ds(pl.multiple_of(q * 8, 8), USED)
         dst[mine, :] = src[0:USED, :] if shared else src[mine, :]
         every = dst.at[pl.ds(0, (Q - 1) * USED), :]
@@ -363,21 +371,36 @@
 
     def gather_start(n):
         settle(2 + 4 * n, "in")
-        for r in range(RR + n):
+        for r in range(RR):
             part = qr[n, pl.ds(r, Q, stride=8), :]
             zb[n, r] = part
             zr[n, r, zmine, :] = part
-        used = pl.ds(0, RR + n)
         z_start(
-            3 + 4 * n, lambda t: zb.at[n, used], zr.at[n, used, zmine, :],
-            zr.at[n, used, pl.ds(0, (Z - 1) * Q), :],
+            3 + 4 * n, lambda t: zb.at[n], zr.at[n, :, zmine, :],
+            zr.at[n, :, pl.ds(0, (Z - 1) * Q), :],
         )
+        if n == 1:
+            row = qr[n, pl.ds(RR, Q, stride=8), :].sum(axis=0, keepdims=True)
+            row_start(0, row)
+
+    def row_start(i, row):
+        row = jnp.broadcast_to(row, (8, LANES))
+        eb[i] = row
+        er[i, z] = row
+        z_start(14 + i, lambda t: eb.at[i], er.at[i, z], er.at[i, pl.ds(0, Z - 1)])
+
+    def row_finish(i):
+        settle(14 + i, "in")
+        tot = er[i, 0]
+        for t in range(1, Z):
+            tot = tot + er[i, t]
+        return tot
 
     def gather_wait(n):
         settle(3 + 4 * n, "in")
 
     def own_step(n):
-        tot = jnp.broadcast_to(zr[n, RR].sum(axis=0, keepdims=True), (8, LANES))
+        tot = row_finish(0)
         below = pltpu.roll(tot, LANES - CG, 1)
         row = jnp.where(lane8 < CG, tot / below, jnp.float32(0.0))
         for shift in (8, 16, 32, 64):
@@ -427,28 +450,29 @@
         if n == 1:
             mine = xf0[pl.ds(pl.multiple_of(z * NFZ, 8) if NFZ % 8 == 0 else z * NFZ, NFZ), :]
             energy = (mine * y).sum(axis=0, keepdims=True)
-            ob[n, RR] = jnp.where(la == 0, energy, jnp.float32(0.0))
-        used = pl.ds(0, RR + n)
+            energy = jnp.where(la[0:1] == 0, energy, jnp.float32(0.0))
         zs = (zs0, zs1)[n]
-        zs[z, used] = ob[n, used, zmine, :]
+        zs[z] = ob[n, :, zmine, :]
         z_start(
             4 + 4 * n,
-            lambda t: ob.at[n, used, pl.ds(pl.multiple_of(t * Q, Q), Q), :],
-            zs.at[z, used],
-            zs.at[pl.ds(0, Z - 1), used],
+            lambda t: ob.at[n, :, pl.ds(pl.multiple_of(t * Q, Q), Q), :],
+            zs.at[z],
+            zs.at[pl.ds(0, Z - 1)],
         )
+        if n == 1:
+            row_start(1, energy)
 
     def backward_start(n):
         zs = (zs0, zs1)[n]
         settle(4 + 4 * n, "in")
         b = qb.at[2 + n]
-        for r in range(RR + n):
+        for r in range(RR):
             tot = zs[0, r]
             for t in range(1, Z):
                 tot = tot + zs[t, r]
             b[pl.ds(r, Q, stride=8), :] = tot
-        for r in range(RR + n, RR + 1):
-            b[pl.ds(r, Q, stride=8), :] = jnp.zeros((Q, LANES), F32)
+        last = row_finish(1)[0:1] if n == 1 else jnp.zeros((1, LANES), F32)
+        b[pl.ds(RR, Q, stride=8), :] = jnp.broadcast_to(last, (Q, LANES))
         q_start(5 + 4 * n, b, qr.at[2 + n])
 
     def backward_finish(n):
@@ -702,11 +726,11 @@
             pltpu.VMEM((NCZ, LANES), F32),
             pltpu.VMEM((4, Q * 8, LANES), F32),
             pltpu.VMEM((4, Q * 8, LANES), F32),
-            pltpu.VMEM((2, RR + 1, Q, LANES), F32),
-            pltpu.VMEM((2, RR + 1, ZQ, LANES), F32),
-            pltpu.VMEM((2, RR + 1, ZQ, LANES), F32),
-            pltpu.VMEM((Z, RR + 1, Q, LANES), F32),
-            pltpu.VMEM((Z, RR + 1, Q, LANES), F32),
+            pltpu.VMEM((2, RR, Q, LANES), F32),
+            pltpu.VMEM((2, RR, ZQ, LANES), F32),
+            pltpu.VMEM((2, RR, ZQ, LANES), F32),
+            pltpu.VMEM((Z, RR, Q, LANES), F32),
+            pltpu.VMEM((Z, RR, Q, LANES), F32),
             pltpu.VMEM((5, 8, LANES), F32),
             pltpu.VMEM((3, Q * 8, LANES), F32),
             pltpu.VMEM((Q, LANES), F32),
@@ -716,10 +740,12 @@
             pltpu.SemaphoreType.DMA((3,)),
             pltpu.SemaphoreType.DMA((2,)),
             pltpu.SemaphoreType.DMA((2,)),
-            pltpu.SemaphoreType.DMA((14,)),
-            pltpu.SemaphoreType.DMA((14,)),
+            pltpu.SemaphoreType.DMA((16,)),
+            pltpu.SemaphoreType.DMA((16,)),
             pltpu.SemaphoreType.DMA((10, 2)),
             pltpu.SemaphoreType.DMA((10, 2)),
+            pltpu.VMEM((2, 8, LANES), F32),
+            pltpu.VMEM((2, Z, 8, LANES), F32),
         ],
         compiler_params=pltpu.CompilerParams(
             collective_id=0, has_side_effects=True, vmem_limit_bytes=56 * 1024 * 1024

time: 99.7 us -> 97.6 us (0.979)
  Pallas kernels: 96.4 us -> 94.3 us
    pallas_call x1, Pallas kernels: 96.4 us -> 94.3 us  [shards(): pl.pallas_call(functools.partial(kernel, Q, Z), out_shape=(out, out, out,...]
where the time goes in v6:
time: 97.6 us; the launch traced here: 97.3 us
  Pallas kernels  94.3 us (97%)
  other arithmetic  2.35 us (2%)
    pallas_call x1, Pallas kernels, shards(): pl.pallas_call(functools.partial(kernel, Q, Z), out_shape=(out, out, out,...  94.3 us
    add x1, other arithmetic, shards(): preconditioned + beta * direction  2.35 us

profile of v6, /device:TPU:1, one launch (start us, length us, event | category | flops | bytes accessed | tf_op | source)
XLA Modules:
  0.0 97.3 jit_solution(13364398673044226489)
XLA Ops:
  0.6 94.3 %shard_map.130 = (f32[12,128,256]{2,1,0:T(8,128)S(1)}, f32[12,128,256]{2,1,0:T(8,128)S(1)}, f32[12,128,256]{2,1,0:T(8,128)S(1)}, f32[12,128,256]{2,1,0:T(8,128)S...) custom-call(f32[12,128,256]{2,1,0:T(8,128)} %bitcast.17, f32[1536,768]{1,0:T(8,128)} %bitcast.12, f32[1536,768]{1,0:T(8,128)} %bitcast.13, ...), custom_call_target="tpu_custom_call" | custom-call | tf_op jit(solution)/shard_map/pallas_call | solution.py:691
  95.0 2.3 %multiply_add_fusion = (f32[12,128,256]{2,1,0:T(8,128)}, f32[12,128,256]{2,1,0:T(8,128)}, f32[12,128,256]{2,1,0:T(8,128)}) fusion(f32[12,128,256]{2,1,0:T(8,128)S(1)} %get-tuple-element.13, f32[12,128,256]{2,1,0:T(8,128)S(1)} %get-tuple-element.10, f32[256]{0:T(256)S(1)} %bitcast.11, f32[256]{0:T(256)S(1)} %bitcast.10, ...), kind=kLoop, calls=%fused_computation | loop fusion | flops 1966080 | bytes 11012096 | tf_op jit(solution)/shard_map/add | solution.py:766

commit v7 on v6

--- a/solution.py
+++ b/solution.py
@@ -603,7 +603,6 @@
             x = dot(b, hi)
             gs[place] = 0.5 * (x[:NCL] + x[32:32 + NCL] + dot(b[:32], lo)[:NCL])
     pair_start(5, gs, gr, SUBS)
-    halo_start(2, prod, hs2, hr2)
 
     def image_here(k, acc):
         m = prod[k]
@@ -616,6 +615,7 @@
     for s in range(SUBS):
         loads[s] = loads[s] + gr[place_of(downs[s])[2]] + gr[place_of(ups[s])[2]]
     forward_start(1, loads, [rz_part, da_part])
+    halo_start(2, prod, hs2, hr2)
     sums_start(0, [rz_part, da_part])
     gather_start(1)
     sums_pass(0)

time: 97.6 us -> 98.9 us (1.013)
  Pallas kernels: 94.3 us -> 95.7 us
    pallas_call x1, Pallas kernels: 94.3 us -> 95.7 us  [shards(): pl.pallas_call(functools.partial(kernel, Q, Z), out_shape=(out, out, out,...]
where the time goes in v7:
time: 98.9 us; the launch traced here: 98.7 us
  Pallas kernels  95.7 us (97%)
  other arithmetic  2.35 us (2%)
    pallas_call x1, Pallas kernels, shards(): pl.pallas_call(functools.partial(kernel, Q, Z), out_shape=(out, out, out,...  95.7 us
    add x1, other arithmetic, shards(): preconditioned + beta * direction  2.35 us

profile of v7, /device:TPU:1, one launch (start us, length us, event | category | flops | bytes accessed | tf_op | source)
XLA Modules:
  0.0 98.7 jit_solution(2451152248729436407)
XLA Ops:
  0.6 95.7 %shard_map.130 = (f32[12,128,256]{2,1,0:T(8,128)S(1)}, f32[12,128,256]{2,1,0:T(8,128)S(1)}, f32[12,128,256]{2,1,0:T(8,128)S(1)}, f32[12,128,256]{2,1,0:T(8,128)S...) custom-call(f32[12,128,256]{2,1,0:T(8,128)} %bitcast.17, f32[1536,768]{1,0:T(8,128)} %bitcast.12, f32[1536,768]{1,0:T(8,128)} %bitcast.13, ...), custom_call_target="tpu_custom_call" | custom-call | tf_op jit(solution)/shard_map/pallas_call | solution.py:691
  96.3 2.3 %multiply_add_fusion = (f32[12,128,256]{2,1,0:T(8,128)}, f32[12,128,256]{2,1,0:T(8,128)}, f32[12,128,256]{2,1,0:T(8,128)}) fusion(f32[12,128,256]{2,1,0:T(8,128)S(1)} %get-tuple-element.13, f32[12,128,256]{2,1,0:T(8,128)S(1)} %get-tuple-element.10, f32[256]{0:T(256)S(1)} %bitcast.11, f32[256]{0:T(256)S(1)} %bitcast.10, ...), kind=kLoop, calls=%fused_computation | loop fusion | flops 1966080 | bytes 11012096 | tf_op jit(solution)/shard_map/add | solution.py:766
